TPU v7x, 512 devices: a whole 4x8x8 slice. The times are simulated.
512 devices in a mesh: pipe: 4 (over x), tm: 32 (over y_lo, z), dp: 4 (over y_hi, core).
Axes of the slice: x: 4, y: 8 (y_hi: 2, y_lo: 4; y = y_hi * 4 + y_lo), z: 8, core: 2. Of those that a mesh axis runs over, the one named last changes fastest.
Arguments:
- video: bfloat16 [4, 4, 64, 64, 320], P(None, 'dp', 'tm'), may hold values from -6 to 6
- cotangent: bfloat16 [4, 4, 64, 64, 320], P(None, 'dp', 'tm'), may hold values from -6 to 6
- timesteps: int32 [4, 4], P(None, 'dp'), may hold values from 0 to 999
- conv_weight: bfloat16 [4, 3, 320, 320], P('pipe'), may hold values from -0.1875 to 0.1875
- out_weight: bfloat16 [4, 320, 320], P('pipe'), may hold values from -0.3125 to 0.3125
Outputs:
- conv_grad: float32 [4, 3, 320, 320], P('pipe')
- out_grad: float32 [4, 320, 320], P('pipe')
All inputs are finite; a program needn't handle non-finite values.
Results may differ from a plain program's by a relative error of at most 0.012.
Values may be sent and summed in bfloat16 or wider, within the bound.
A program may use at most 64 MiB of HBM per device.

v0:
```python
import math

import jax
import jax.numpy as jnp
from jax import lax
from jax.sharding import PartitionSpec as P

EPSILON = 1e-06


def padded_2(block, sides, width):
    for axis, dim in sides:
        count = lax.axis_size(axis)
        forward = [(i, i + 1) for i in range(count - 1)]
        backward = [(target, source) for source, target in forward]
        low = lax.ppermute(
            lax.slice_in_dim(block, block.shape[dim] - width, None, axis=dim), axis, forward
        )
        high = lax.ppermute(lax.slice_in_dim(block, 0, width, axis=dim), axis, backward)
        block = jnp.concatenate([low, block, high], axis=dim)
    return block


def from_partner(value, axis, stride):
    mask = 2**stride
    pairs = [(source, source ^ mask) for source in range(lax.axis_size(axis))]
    return lax.ppermute(value, axis, pairs)


def from_behind(array, axis, by):
    peers = lax.axis_size(axis)
    pairs = [(i, i + by) for i in range(peers) if 0 <= i + by < peers]
    return lax.ppermute(array, axis, pairs)


def embed(times, channels):
    half = channels // 2
    index = jnp.arange(half).astype(jnp.float32)
    freq = jnp.exp(index * (-math.log(10000.0) / half))
    angle = times.astype(jnp.float32)[..., None] * freq
    return jnp.concatenate([jnp.sin(angle), jnp.cos(angle)], -1)


def prepare(inputs, emb_pair, conv_pair):
    x_float = inputs.astype(jnp.float32)
    inv_rms = lax.rsqrt(jnp.mean(x_float * x_float, -1, keepdims=True) + EPSILON)
    normed = x_float * inv_rms
    norm_low = normed.astype(jnp.bfloat16)
    padded = padded_2(norm_low, (("tm", 1),), 1)
    frames = inputs.shape[1]
    pre_act = emb_pair[:, None, None, :]
    for offset in range(3):
        pre_act = pre_act + jnp.einsum(
            "dfpc,dcx->dfpx",
            padded[:, offset : offset + frames],
            conv_pair[:, offset],
            preferred_element_type=jnp.float32,
        )
    active = jax.nn.silu(pre_act).astype(jnp.bfloat16)
    return (inv_rms, normed, padded, pre_act, active)


def body(video, cotangent, timesteps, conv_weight, out_weight):
    current_section_index = lax.axis_index("pipe")
    sections = lax.axis_size("pipe")
    final_section = sections - 1
    micro = video.shape[0]
    half_microbatch_count = micro // 2
    ticks = half_microbatch_count + sections - 1
    channels = video.shape[-1]
    frames = video.shape[2]
    bit_count = sections.bit_length() - 1
    packed = jnp.concatenate([conv_weight[0], out_weight[0][None]], 0)
    mirrored = packed
    for bit_pos in range(bit_count):
        mirrored = from_partner(mirrored, "pipe", bit_pos)
    conv_pair = jnp.stack([conv_weight[0], mirrored[:3]])
    out_pair = jnp.stack([out_weight[0], mirrored[3]])
    embedded = embed(timesteps[:, 0], channels)

    def pick(stacked, down_tick, up_tick):
        down_part = lax.dynamic_index_in_dim(
            stacked, jnp.clip(down_tick, 0, ticks - 1), 0, keepdims=False
        )[0]
        up_part = lax.dynamic_index_in_dim(
            stacked, jnp.clip(up_tick, 0, ticks - 1), 0, keepdims=False
        )[1]
        return jnp.stack([down_part, up_part])

    empty_activation = jnp.zeros(video.shape[2:], jnp.bfloat16)
    down_buf = empty_activation
    up_buf = empty_activation
    saved = []
    for current_clock_tick in range(ticks):
        down_in = down_buf
        up_in = up_buf
        if current_clock_tick < half_microbatch_count:
            down_in = jnp.where(current_section_index == 0, video[current_clock_tick, 0], down_buf)
            up_in = jnp.where(
                current_section_index == final_section,
                video[half_microbatch_count + current_clock_tick, 0],
                up_buf,
            )
        inputs = jnp.stack([down_in, up_in])
        down_row = lax.dynamic_index_in_dim(
            embedded,
            jnp.clip(current_clock_tick - current_section_index, 0, half_microbatch_count - 1),
            0,
            keepdims=False,
        )
        up_row = lax.dynamic_index_in_dim(
            embedded,
            half_microbatch_count
            + jnp.clip(
                current_clock_tick - (final_section - current_section_index),
                0,
                half_microbatch_count - 1,
            ),
            0,
            keepdims=False,
        )
        emb_pair = jnp.stack([down_row, up_row])
        inv_rms, normed, padded, pre_act, active = prepare(inputs, emb_pair, conv_pair)
        outputs = (
            inputs.astype(jnp.float32)
            + jnp.einsum("dfpc,dcx->dfpx", active, out_pair, preferred_element_type=jnp.float32)
        ).astype(jnp.bfloat16)
        saved.append((inv_rms, normed, padded, pre_act, active))
        if current_clock_tick + 1 < ticks:
            down_buf = from_behind(outputs[0], "pipe", 1)
            up_buf = from_behind(outputs[1], "pipe", -1)
    stored = jax.tree.map(lambda *leaves: jnp.stack(leaves), *saved)
    conv_acc = jnp.zeros((2, 3, channels, channels), jnp.float32)
    out_acc = jnp.zeros((2, channels, channels), jnp.float32)
    downward_gradient_holder = empty_activation
    upward_gradient_holder = empty_activation
    for current_clock_tick in range(ticks):
        down_micro = current_clock_tick - (final_section - current_section_index)
        up_micro = current_clock_tick - current_section_index
        down_valid = (down_micro >= 0) & (down_micro < half_microbatch_count)
        up_valid = (up_micro >= 0) & (up_micro < half_microbatch_count)
        downward_hidden_gradient = downward_gradient_holder
        upward_hidden_gradient = upward_gradient_holder
        if current_clock_tick < half_microbatch_count:
            downward_hidden_gradient = jnp.where(
                current_section_index == final_section,
                cotangent[current_clock_tick, 0],
                downward_gradient_holder,
            )
            upward_hidden_gradient = jnp.where(
                current_section_index == 0,
                cotangent[half_microbatch_count + current_clock_tick, 0],
                upward_gradient_holder,
            )
        downward_hidden_gradient = jnp.where(down_valid, downward_hidden_gradient, empty_activation)
        upward_hidden_gradient = jnp.where(up_valid, upward_hidden_gradient, empty_activation)
        grad_out = jnp.stack([downward_hidden_gradient, upward_hidden_gradient])
        down_tick = down_micro + current_section_index
        up_tick = up_micro + final_section - current_section_index
        inv_rms, normed, padded, pre_act, active = tuple(
            (pick(item, down_tick, up_tick) for item in stored)
        )
        out_acc = out_acc + jnp.einsum(
            "dfpc,dfpx->dcx", active, grad_out, preferred_element_type=jnp.float32
        )
        grad_act = jnp.einsum(
            "dfpx,dcx->dfpc", grad_out, out_pair, preferred_element_type=jnp.float32
        )
        sigma = jax.nn.sigmoid(pre_act)
        grad_pre = (grad_act * sigma * (1.0 + pre_act * (1.0 - sigma))).astype(jnp.bfloat16)
        grad_pad = padded_2(grad_pre, (("tm", 1),), 1)
        conv_terms = []
        grad_norm = jnp.zeros(normed.shape, jnp.float32)
        for offset in range(3):
            conv_terms.append(
                jnp.einsum(
                    "dfpc,dfpx->dcx",
                    padded[:, offset : offset + frames],
                    grad_pre,
                    preferred_element_type=jnp.float32,
                )
            )
            grad_norm = grad_norm + jnp.einsum(
                "dfpx,dcx->dfpc",
                grad_pad[:, 2 - offset : 2 - offset + frames],
                conv_pair[:, offset],
                preferred_element_type=jnp.float32,
            )
        conv_acc = conv_acc + jnp.stack(conv_terms, 1)
        incoming_gradient = grad_out.astype(jnp.float32) + inv_rms * (
            grad_norm - normed * jnp.mean(grad_norm * normed, -1, keepdims=True)
        )
        incoming_gradient = incoming_gradient.astype(jnp.bfloat16)
        if current_clock_tick + 1 < ticks:
            downward_gradient_holder = from_behind(incoming_gradient[0], "pipe", -1)
            upward_gradient_holder = from_behind(incoming_gradient[1], "pipe", 1)
    down_total = jnp.concatenate([conv_acc[0], out_acc[0][None]], 0)
    up_total = jnp.concatenate([conv_acc[1], out_acc[1][None]], 0)
    down_sum, up_sum = lax.psum((down_total, up_total), ("tm", "dp"))
    value = up_sum
    for bit_pos in range(bit_count):
        value = from_partner(value.astype(jnp.bfloat16), "pipe", bit_pos).astype(value.dtype)
    total = down_sum + value
    row_count = (
        micro * video.shape[1] * lax.axis_size("dp") * frames * lax.axis_size("tm") * video.shape[3]
    )
    scale = 1.0 / math.sqrt(row_count)
    return ((total[:3] * scale)[None], (total[3] * scale)[None])


def solution(mesh):
    return jax.shard_map(
        body,
        mesh=mesh,
        in_specs=(
            P(None, "dp", "tm", None, None),
            P(None, "dp", "tm", None, None),
            P(None, "dp"),
            P("pipe", None, None, None),
            P("pipe", None, None),
        ),
        out_specs=(P("pipe", None, None, None), P("pipe", None, None)),
        check_vma=False,
    )
```

profile of v0, /device:TPU:1, one launch (start us, length us, event | category | flops | bytes accessed | tf_op | source)
XLA Modules:
  0.0 1157.8 jit_solution(2011999744393750065)
XLA Ops:
  7.2 1.0 slice_select_fusion.1
  8.5 1.3 collective-permute-start.1
  9.8 5.5 collective-permute-start
  15.3 1.4 pad_maximum_fusion.2
  16.7 3.3 collective-permute-start.2
  20.5 16.1 %collective-permute-done.2 = bf16[4,320,320]{2,1,0:T(8,128)(2,1)} collective-permute-done((bf16[4,320,320]{2,1,0:T(8,128)(2,1)S(1)}, bf16[4,320,320]{2,1,0:T(8,128)(2,1)}, u32[]{:S(2)}, u32[]{:S(2)}) %collective-permute-start.2) | collective-permute-done | bytes 819232 | tf_op jit(solution)/shard_map/ppermute | solution.py:27
  36.5 9.3 collective-permute-start.3
  46.2 19.5 %collective-permute-done.3 = bf16[4,320,320]{2,1,0:T(8,128)(2,1)S(1)} collective-permute-done((bf16[4,320,320]{2,1,0:T(8,128)(2,1)}, bf16[4,320,320]{2,1,0:T(8,128)(2,1)S(1)}, u32[]{:S(2)}, u32[]{:S(2)}) %collective-permute-start.3) | collective-permute-done | bytes 819232 | tf_op jit(solution)/shard_map/ppermute | solution.py:27
  69.6 1.8 collective-permute-start.4
  71.4 1.3 collective-permute-start.5
  73.0 5.3 collective-permute-done.5
  78.9 4.0 collective-permute-start.6
  83.0 1.3 collective-permute-start.7
  84.8 4.5 collective-permute-done.7
  90.0 3.4 collective-permute-start.8
  93.4 1.3 collective-permute-start.9
  95.0 3.7 collective-permute-done.9
  99.3 5.2 collective-permute-start.10
  104.7 1.3 collective-permute-start.11
  106.5 3.6 collective-permute-done.11
  110.8 2.8 collective-permute-start.12
  113.6 1.3 collective-permute-start.13
  115.2 3.7 collective-permute-done.13
  119.5 4.0 collective-permute-start.14
  123.6 1.3 collective-permute-start.15
  125.4 3.6 collective-permute-done.15
  129.7 2.0 collective-permute-start.16
  131.8 1.3 collective-permute-start.17
  133.4 3.7 collective-permute-done.17
  137.7 1.3 collective-permute-start.19
  139.0 4.0 collective-permute-start.18
  143.4 1.3 collective-permute-done.18
  147.2 3.7 collective-permute-start.21
  151.3 1.5 collective-permute-start.20
  153.1 4.4 collective-permute-done.20
  158.1 1.3 collective-permute-start.22
  159.4 4.0 collective-permute-start.23
  163.6 1.5 collective-permute-done.23
  166.1 4.6 collective-permute-start.25
  171.7 1.3 collective-permute-start.24
  173.3 5.3 collective-permute-done.24
  179.3 1.3 collective-permute-start.26
  180.9 4.4 collective-permute-start.27
  185.3 1.6 collective-permute-done.27
  188.0 4.6 collective-permute-start.29
  192.8 1.3 collective-permute-start.28
  194.5 3.7 collective-permute-done.28
  198.8 1.3 collective-permute-start.30
  200.5 4.7 collective-permute-start.31
  205.2 1.6 collective-permute-done.31
  207.8 3.8 collective-permute-start.33
  211.9 1.3 collective-permute-start.32
  213.9 5.3 collective-permute-done.32
  219.8 1.3 collective-permute-start.34
  221.8 4.8 collective-permute-start.35
  226.8 1.9 collective-permute-done.35
  232.9 670.0 %all-reduce.4 = bf16[4,320,320]{2,1,0:T(8,128)(2,1)} all-reduce(f32[4,320,320]{2,1,0:T(8,128)S(1)} %pad_maximum_fusion.1), channel_id=1, replica_groups=mesh['pipe'=4,'tm'=32,'dp'=4] {'tm','dp'}, use_global_device_ids=true, to_apply=%region_10.11 | all-reduce | flops 409600 | bytes 2457600 | tf_op jit(solution)/shard_map/psum | solution.py:199
  903.0 3.4 collective-permute-start.36
  906.4 2.5 pad_maximum_fusion
  908.8 19.9 %collective-permute-done.36 = bf16[4,320,320]{2,1,0:T(8,128)(2,1)S(1)} collective-permute-done((bf16[4,320,320]{2,1,0:T(8,128)(2,1)}, bf16[4,320,320]{2,1,0:T(8,128)(2,1)S(1)}, u32[]{:S(2)}, u32[]{:S(2)}) %collective-permute-start.36) | collective-permute-done | bytes 819232 | tf_op jit(solution)/shard_map/ppermute | solution.py:27
  928.7 5.8 collective-permute-start.37
  934.6 212.7 %all-reduce.3.cloned.1.call-done = f32[4,320,320]{2,1,0:T(8,128)} async-done(((f32[4,320,320]{2,1,0:T(8,128)}), f32[4,320,320]{2,1,0:T(8,128)}) %all-reduce.3.cloned.1.call-update) | async-done | bytes 1638416 | tf_op jit(solution)/shard_map/psum | solution.py:199
  1147.2 1.7 convert_add_fusion
  1149.8 1.2 fusion.3
  (185 shorter events, 30.5 us)
Async XLA Ops:
  7.2 12.9 %copy-start.5 = (s32[4,1]{0,1:T(1,128)S(1)}, s32[4,1]{0,1:T(1,128)}, u32[]{:S(2)}) copy-start(s32[4,1]{0,1:T(1,128)} %param.7) | copy-start | bytes 52
  7.2 38.8 %copy-start.3 = (bf16[4,1,2,64,320]{4,3,2,1,0:T(8,128)(2,1)S(1)}, bf16[4,1,2,64,320]{4,3,2,1,0:T(8,128)(2,1)}, u32[]{:S(2)}) copy-start(bf16[4,1,2,64,320]{4,3,2,1,0:T(8,128)(2,1)} %param.6) | copy-start | bytes 983044
  7.2 1140.1 %all-reduce.3.cloned.1.call-start = ((), (), s32[]{:S(2)}) async-start(), calls=%async_computation | async-start | bytes 3932160 | tf_op jit(solution)/shard_map/psum | solution.py:199
  8.5 37.6 %collective-permute-start.1 = (bf16[2,1,64,320]{3,2,1,0:T(8,128)(2,1)S(1)}, bf16[2,1,64,320]{3,2,1,0:T(8,128)(2,1)S(1)}, u32[]{:S(2)}, u32[]{:S(2)}) collective-permute-start(bf16[2,1,64,320]{3,2,1,0:T(8,128)(2,1)S(1)} %get-tuple-element.91), channel_id=1, source_target_pairs={{4,0},{8,4},{12,8},{16,12},{20,16},{24,20},{28,24},{32,28},{36,32}... | collective-permute-start | bytes 245768 | tf_op jit(solution)/shard_map/ppermute | solution.py:19
  9.8 36.3 %collective-permute-start = (bf16[2,1,64,320]{3,2,1,0:T(8,128)(2,1)S(1)}, bf16[2,1,64,320]{3,2,1,0:T(8,128)(2,1)S(1)}, u32[]{:S(2)}, u32[]{:S(2)}) collective-permute-start(bf16[2,1,64,320]{3,2,1,0:T(8,128)(2,1)S(1)} %get-tuple-element.92), channel_id=1, source_target_pairs={{0,4},{4,8},{8,12},{12,16},{16,20},{20,24},{24,28},{28,32},{32,36}... | collective-permute-start | bytes 245768 | tf_op jit(solution)/shard_map/ppermute | solution.py:16
  16.7 49.9 %copy-start = (bf16[1,3,320,320]{3,2,1,0:T(8,128)(2,1)S(1)}, bf16[1,3,320,320]{3,2,1,0:T(8,128)(2,1)}, u32[]{:S(2)}) copy-start(bf16[1,3,320,320]{3,2,1,0:T(8,128)(2,1)} %param.8) | copy-start | bytes 1843204
  16.7 19.8 %collective-permute-start.2 = (bf16[4,320,320]{2,1,0:T(8,128)(2,1)S(1)}, bf16[4,320,320]{2,1,0:T(8,128)(2,1)}, u32[]{:S(2)}, u32[]{:S(2)}) collective-permute-start(bf16[4,320,320]{2,1,0:T(8,128)(2,1)S(1)} %pad_maximum_fusion.2), channel_id=1, source_target_pairs={{0,128},{128,0},{256,384},{384,256},{1,129},{129,1},{257,385},{385... | collective-permute-start | bytes 2457608 | tf_op jit(solution)/shard_map/ppermute | solution.py:27
  36.5 29.2 %collective-permute-start.3 = (bf16[4,320,320]{2,1,0:T(8,128)(2,1)}, bf16[4,320,320]{2,1,0:T(8,128)(2,1)S(1)}, u32[]{:S(2)}, u32[]{:S(2)}) collective-permute-start(bf16[4,320,320]{2,1,0:T(8,128)(2,1)} %collective-permute-done.2), channel_id=1, source_target_pairs={{0,256},{128,384},{256,0},{384,128},{1,257},{129,385},{257,1},{385... | collective-permute-start | bytes 2457608 | tf_op jit(solution)/shard_map/ppermute | solution.py:27
  65.7 0.9 copy-start.1
  68.2 0.9 copy-start.4
  69.2 9.1 copy-start.2
  69.6 3.4 collective-permute-start.4
  71.4 6.9 collective-permute-start.5
  78.9 5.6 collective-permute-start.6
  83.0 6.2 collective-permute-start.7
  90.0 5.0 collective-permute-start.8
  93.4 5.4 collective-permute-start.9
  99.3 6.8 collective-permute-start.10
  104.7 5.4 collective-permute-start.11
  110.8 4.4 collective-permute-start.12
  113.6 5.4 collective-permute-start.13
  119.5 5.6 collective-permute-start.14
  123.6 5.4 collective-permute-start.15
  129.7 3.6 collective-permute-start.16
  131.8 5.4 collective-permute-start.17
  137.7 7.2 collective-permute-start.19
  139.0 5.6 collective-permute-start.18
  147.2 5.5 collective-permute-start.21
  151.3 6.2 collective-permute-start.20
  158.1 5.5 collective-permute-start.22
  159.4 5.6 collective-permute-start.23
  166.1 6.9 collective-permute-start.25
  171.7 6.9 collective-permute-start.24
  179.3 6.0 collective-permute-start.26
  180.9 6.0 collective-permute-start.27
  188.0 6.2 collective-permute-start.29
  192.8 5.4 collective-permute-start.28
  198.8 6.3 collective-permute-start.30
  200.5 6.3 collective-permute-start.31
  207.8 5.8 collective-permute-start.33
  211.9 7.3 collective-permute-start.32
  219.8 7.0 collective-permute-start.34
  221.8 6.9 collective-permute-start.35
  903.0 25.8 %collective-permute-start.36 = (bf16[4,320,320]{2,1,0:T(8,128)(2,1)}, bf16[4,320,320]{2,1,0:T(8,128)(2,1)S(1)}, u32[]{:S(2)}, u32[]{:S(2)}) collective-permute-start(bf16[4,320,320]{2,1,0:T(8,128)(2,1)} %all-reduce.4), channel_id=1, source_target_pairs={{0,128},{128,0},{256,384},{384,256},{1,129},{129,1},{257,385},{385... | collective-permute-start | bytes 2457608 | tf_op jit(solution)/shard_map/ppermute | solution.py:27
  928.7 218.5 %collective-permute-start.37 = (bf16[4,320,320]{2,1,0:T(8,128)(2,1)S(1)}, bf16[4,320,320]{2,1,0:T(8,128)(2,1)S(1)}, u32[]{:S(2)}, u32[]{:S(2)}) collective-permute-start(bf16[4,320,320]{2,1,0:T(8,128)(2,1)S(1)} %collective-permute-done.36), channel_id=1, source_target_pairs={{0,256},{128,384},{256,0},{384,128},{1,257},{129,385},{257,1},{385... | collective-permute-start | bytes 2457608 | tf_op jit(solution)/shard_map/ppermute | solution.py:27
Sparse Core Ops, SparseCore 0:
  909.0 238.2 all-reduce.2
where the time goes:
time: 1160 us
  blocking collectives  670 us (58%)
  waiting for transfers between devices  325 us (28%)
  starting transfers between devices  111 us (10%)
  matrix products  18.2 us (2%)
  between operations  15.5 us (1%)
  other arithmetic  13.4 us (1%)
    psum x1, blocking collectives, body(): down_sum, up_sum = lax.psum((down_total, up_total), ('tm', 'dp'))  670 us
    psum x1, waiting for transfers between devices, body(): down_sum, up_sum = lax.psum((down_total, up_total), ('tm', 'dp'))  213 us
    ppermute x4, waiting for transfers between devices, from_partner(): return lax.ppermute(value, axis, pairs)  55.5 us
    ppermute x9, starting transfers between devices, padded_2(): lax.ppermute(lax.slice_in_dim(block, block.shape[dim] - width, None, axis...  39.3 us
    ppermute x16, starting transfers between devices, from_behind(): return lax.ppermute(array, axis, pairs)  38.2 us
    ppermute x9, waiting for transfers between devices, padded_2(): lax.ppermute(lax.slice_in_dim(block, 0, width, axis=dim), axis, backward)  30.4 us
    ppermute x16, waiting for transfers between devices, from_behind(): return lax.ppermute(array, axis, pairs)  24.1 us
  transfers between devices with their start and end apart: 39, of which 29 were waited for; matrix products, arithmetic and copies ran while one was open for 1% of the time, Pallas kernels for 0%

commit v1 on v0

v1 whole, which is shorter than its diff:
```python
import functools
import math

import jax
import jax.numpy as jnp
from jax import lax
from jax.experimental import pallas as pl
from jax.experimental.pallas import tpu as pltpu
from jax.sharding import PartitionSpec as P

EPSILON = 1e-06
MESH = pl.DeviceIdType.MESH
SECTIONS = 4
C = 320
ROWS = 128
YL, Z, Y = 4, 8, 8
PA, PB = 112, 96
HA, HB = 8 * PA, 8 * PB
TOTAL = 2 * (HA + HB)
BF = jnp.bfloat16
F32 = jnp.float32


def place():
    p, t, d = lax.axis_index("pipe"), lax.axis_index("tm"), lax.axis_index("dp")
    return p, lax.div(d, 2) * YL + lax.div(t, Z), lax.rem(t, Z), lax.rem(d, 2)


def device(p, y, z, c):
    return (p, lax.rem(y, YL) * Z + z, lax.div(y, YL) * 2 + c)


def remote(src, dst, send, recv, to):
    return pltpu.make_async_remote_copy(
        src_ref=src, dst_ref=dst, send_sem=send, recv_sem=recv, device_id=to, device_id_type=MESH
    )


def each(count, fn):
    def step(i, _):
        fn(i)
        return 0

    lax.fori_loop(1, count, step, 0)


def dot(a, b):
    return jnp.dot(a, b, preferred_element_type=F32)


def dot_t(a, b):
    return lax.dot_general(a, b, (((1,), (1,)), ((), ())), preferred_element_type=F32)


def t_dot(a, b):
    return lax.dot_general(a, b, (((0,), (0,)), ((), ())), preferred_element_type=F32)


def normalize(h):
    x = h.astype(F32)
    inv = lax.rsqrt(jnp.mean(x * x, -1, keepdims=True) + EPSILON)
    return x, inv, x * inv


def before(v):
    row = lax.rem(lax.broadcasted_iota(jnp.int32, v.shape, 0), ROWS)
    return jnp.where(row < 2, 0.0, pltpu.roll(v, 2, 0))


def after(v):
    row = lax.rem(lax.broadcasted_iota(jnp.int32, v.shape, 0), ROWS)
    return jnp.where(row >= ROWS - 2, 0.0, pltpu.roll(v, v.shape[0] - 2, 0))


def reorder(source_of, v):
    r = lax.broadcasted_iota(jnp.int32, (ROWS, ROWS), 0)
    k = lax.broadcasted_iota(jnp.int32, (ROWS, ROWS), 1)
    pick = jnp.where(source_of(r) == k, 1.0, 0.0).astype(BF)
    return dot(pick, v).astype(BF)


def to_z(r):
    return lax.rem(lax.div(r, 8), 2) * 64 + lax.div(r, 16) * 8 + lax.rem(r, 8)


def to_y(r):
    return lax.div(lax.rem(r, 32), 2) * 8 + lax.div(r, 32) * 2 + lax.rem(r, 2)


def chain_kernel(
    video, cotangent, emb, convw, outw, g_ref,
    vin, cin, w, s1s, s1d, s2s, s2d, hs, ds, pre_s, hr, dr, nb, ab, d0, d1, d2,
    in_sem, z_send, z_recv, y_send, y_recv,
    x_send, x_recv, f_send, f_recv, q_send, q_recv, c_send, c_recv,
    h_send, h_recv, d_send, d_recv,
):
    p, y, z, c = place()
    yl = lax.rem(y, YL)
    ybase = y - yl
    loads = [
        pltpu.make_async_copy(video.at[p, 0], vin, in_sem.at[0]),
        pltpu.make_async_copy(cotangent.at[p, 0], cin, in_sem.at[1]),
        pltpu.make_async_copy(convw.at[0], w.at[p, pl.ds(0, 3)], in_sem.at[2]),
        pltpu.make_async_copy(outw.at[0], w.at[p, 3], in_sem.at[3]),
    ]
    for load in loads:
        load.start()

    barrier = pltpu.get_barrier_semaphore()

    def greet(to):
        pl.semaphore_signal(barrier, inc=1, device_id=to, device_id_type=MESH)

    each(SECTIONS, lambda i: greet(device(lax.rem(p + i, SECTIONS), y, z, c)))
    each(Z, lambda i: greet(device(p, y, lax.rem(z + i, Z), c)))
    each(YL, lambda i: greet(device(p, ybase + lax.rem(yl + i, YL), z, c)))
    greet(device(p, y, z, 1 - c))
    for load in loads:
        load.wait()
    pl.semaphore_wait(barrier, SECTIONS + Z + YL - 3 + 1)

    right, left = lax.rem(p + 1, SECTIONS), lax.rem(p + 3, SECTIONS)
    far = lax.rem(p + 2, SECTIONS)
    odd = jnp.where(c == 0, lax.rem(z, 2), lax.rem(y, 2))
    mine, theirs = 2 * c + odd, 2 * c + 1 - odd
    hop = 1 - 2 * odd
    pair = device(p, y + hop * c, z + hop * (1 - c), c)
    other = device(p, y, z, 1 - c)
    to_right, to_left = device(right, y, z, c), device(left, y, z, c)
    half = [pl.ds(0, C // 2), pl.ds(C // 2, C // 2)]

    def over_x(section, part, way, target):
        ref = w.at[section, mine, half[part]]
        return remote(ref, ref, x_send.at[way, part], x_recv.at[section, part], target)

    def forward(section, part, way, target):
        ref = w.at[section, mine, half[part]]
        return remote(ref, ref, f_send.at[way], f_recv.at[part], target)

    def to_pair(section, matrix):
        ref = w.at[section, matrix]
        return remote(ref, ref, q_send.at[section], q_recv.at[section], pair)

    def to_core(section, matrix):
        ref = w.at[section, matrix]
        return remote(ref, ref, c_send.at[section, matrix], c_recv.at[section, matrix], other)

    over_x(p, 0, 0, to_right).start()
    over_x(p, 1, 1, to_left).start()
    over_x(p, 1, 0, to_right).start()
    over_x(p, 0, 1, to_left).start()

    s1s[:, 0:16, :] = reorder(to_z, vin[...].reshape(ROWS, C)).reshape(Z, 16, C)
    s1s[:, 16:32, :] = reorder(to_z, cin[...].reshape(ROWS, C)).reshape(Z, 16, C)

    def z_copy(at, slot):
        return remote(s1s.at[at], s1d.at[slot], z_send.at[at], z_recv.at[slot], device(p, y, at, c))

    each(Z, lambda i: z_copy(lax.rem(z + i, Z), z).start())
    s1d[z] = s1s[z]

    over_x(left, 0, 0, to_right).wait_recv()
    forward(left, 0, 0, to_right).start()
    over_x(right, 1, 1, to_left).wait_recv()
    forward(right, 1, 1, to_left).start()

    each(Z, lambda i: z_copy(lax.rem(z + i, Z), lax.rem(z + i, Z)).wait_recv())
    s2s[:, 0:32, :] = reorder(to_y, s1d[:, 0:16, :].reshape(ROWS, C)).reshape(YL, 32, C)
    s2s[:, 32:64, :] = reorder(to_y, s1d[:, 16:32, :].reshape(ROWS, C)).reshape(YL, 32, C)

    def y_copy(at, slot):
        return remote(s2s.at[at], s2d.at[slot], y_send.at[at], y_recv.at[slot], device(p, ybase + at, z, c))

    each(YL, lambda i: y_copy(lax.rem(yl + i, YL), yl).start())
    s2d[yl] = s2s[yl]

    over_x(left, 1, 0, to_right).wait_recv()
    to_pair(left, mine).start()
    to_core(left, mine).start()
    over_x(right, 0, 1, to_left).wait_recv()
    to_pair(right, mine).start()
    to_core(right, mine).start()

    each(YL, lambda i: y_copy(lax.rem(yl + i, YL), lax.rem(yl + i, YL)).wait_recv())
    hs[0] = s2d[:, 0:32, :].reshape(ROWS, C)
    ds[3] = s2d[:, 32:64, :].reshape(ROWS, C)

    def give(value, kept, send, recv, section):
        copy = remote(value.at[section], kept.at[p], send.at[section], recv.at[p], device(section, y, z, c))

        @pl.when(p != section)
        def _():
            copy.start()

        @pl.when(p == section)
        def _():
            kept[p] = value[section]

    give(hs, hr, h_send, h_recv, 0)
    give(ds, dr, d_send, d_recv, 3)

    forward(far, 0, 0, to_right).wait_recv()
    forward(far, 1, 1, to_left).wait_recv()
    to_pair(far, mine).start()
    to_core(far, mine).start()
    for section in (left, right, far):
        to_pair(section, theirs).wait_recv()
        to_core(section, theirs).start()
    for section in (left, right, far):
        to_core(section, 2 * (1 - c)).wait_recv()
        to_core(section, 2 * (1 - c) + 1).wait_recv()

    emb_row = emb[pl.ds(p, 1), :]
    for s in range(SECTIONS):
        x, inv, normed = normalize(hs[s])
        pre = emb_row + dot(before(normed).astype(BF), w[s, 0])
        pre = pre + dot(normed.astype(BF), w[s, 1])
        pre = pre + dot(after(normed).astype(BF), w[s, 2])
        pre_s[s] = pre
        if s + 1 < SECTIONS:
            act = (pre * jax.nn.sigmoid(pre)).astype(BF)
            hs[s + 1] = (x + dot(act, w[s, 3])).astype(BF)
            give(hs, hr, h_send, h_recv, s + 1)
    for s in (3, 2, 1):
        x, inv, normed = normalize(hs[s])
        grad = ds[s]
        pre = pre_s[s]
        sig = jax.nn.sigmoid(pre)
        dpre = dot_t(grad, w[s, 3]) * sig * (1.0 + pre * (1.0 - sig))
        dnorm = dot_t(after(dpre).astype(BF), w[s, 0])
        dnorm = dnorm + dot_t(dpre.astype(BF), w[s, 1])
        dnorm = dnorm + dot_t(before(dpre).astype(BF), w[s, 2])
        mean = jnp.mean(dnorm * normed, -1, keepdims=True)
        ds[s - 1] = (grad.astype(F32) + inv * (dnorm - normed * mean)).astype(BF)
        give(ds, dr, d_send, d_recv, s - 1)

    def take(kept, value, send, recv):
        def one(i):
            m = lax.rem(p + i, SECTIONS)
            remote(value.at[0], kept.at[m], send.at[0], recv.at[m], device(m, y, z, c)).wait_recv()

        each(SECTIONS, one)

    take(hr, hs, h_send, h_recv)

    def redo(m, _):
        x, inv, normed = normalize(hr[m])
        low = normed.astype(BF)
        pre = emb[pl.ds(m, 1), :] + dot(before(normed).astype(BF), w[p, 0])
        pre = pre + dot(low, w[p, 1])
        pre = pre + dot(after(normed).astype(BF), w[p, 2])
        pre_s[m] = pre
        nb[m] = low
        ab[m] = (pre * jax.nn.sigmoid(pre)).astype(BF)
        return 0

    lax.fori_loop(0, SECTIONS, redo, 0)
    take(dr, ds, d_send, d_recv)

    def redo_back(m, _):
        pre = pre_s[m]
        sig = jax.nn.sigmoid(pre)
        dpre = dot_t(dr[m], w[p, 3]) * sig * (1.0 + pre * (1.0 - sig))
        d0[m] = after(dpre).astype(BF)
        d1[m] = dpre.astype(BF)
        d2[m] = before(dpre).astype(BF)
        return 0

    lax.fori_loop(0, SECTIONS, redo_back, 0)
    left_hand = (nb, nb, nb, ab)
    right_hand = (d0, d1, d2, dr)
    tails = []
    for k in range(4):
        term = t_dot(
            left_hand[k][...].reshape(SECTIONS * ROWS, C), right_hand[k][...].reshape(SECTIONS * ROWS, C)
        )
        g_ref[pl.ds(2 * k * C, C), :] = term[:, 0:128]
        g_ref[pl.ds((2 * k + 1) * C, C), :] = term[:, 128:256]
        tails.append(term[:, 256:320])
    g_ref[pl.ds(8 * C, C), :] = jnp.concatenate(tails[0:2], 1)
    g_ref[pl.ds(9 * C, C), :] = jnp.concatenate(tails[2:4], 1)
    g_ref[pl.ds(10 * C, TOTAL - 10 * C), :] = jnp.zeros((TOTAL - 10 * C, 128), F32)

    for part in range(2):
        over_x(p, part, 0, to_right).wait_send()
        over_x(p, part, 1, to_left).wait_send()
    forward(left, 0, 0, to_right).wait_send()
    forward(right, 1, 1, to_left).wait_send()
    for section in (left, right, far):
        to_pair(section, mine).wait_send()
        to_core(section, mine).wait_send()
        to_core(section, theirs).wait_send()
    each(Z, lambda i: z_copy(lax.rem(z + i, Z), z).wait_send())
    each(YL, lambda i: y_copy(lax.rem(yl + i, YL), yl).wait_send())

    def left_us(i):
        s = lax.rem(p + i, SECTIONS)
        to = device(s, y, z, c)
        remote(hs.at[s], hr.at[p], h_send.at[s], h_recv.at[p], to).wait_send()
        remote(ds.at[s], dr.at[p], d_send.at[s], d_recv.at[p], to).wait_send()

    each(SECTIONS, left_us)


def sum_kernel(
    scale, g, conv_out, out_out,
    sb, rb, chip, ra, rbz, ra2, rb2, fin,
    core_sem, a1s, a1r, b1s, b1r, a2s, a2r, b2s, b2r, a3s, a3r, b3s, b3r, end_sem,
):
    p, y, z, c = place()
    other = 1 - c
    sibling = device(p, y, z, other)
    barrier = pltpu.get_barrier_semaphore()

    def greet(to):
        pl.semaphore_signal(barrier, inc=1, device_id=to, device_id_type=MESH)

    def at_y(to):
        return device(p, to, z, c)

    def at_z(to):
        return device(p, y, to, c)

    def y_of(i):
        return lax.rem(y + i, Y)

    def z_of(i):
        return lax.rem(z + i, Z)

    each(Y, lambda i: greet(at_y(y_of(i))))
    each(Z, lambda i: greet(at_z(z_of(i))))
    greet(sibling)

    def rows(start, size):
        return pl.ds(pl.multiple_of(start, 16), size)

    sb[0:HA, :] = g[rows(other * HA, HA), :].astype(BF)
    sb[HA : HA + HB, :] = g[rows(2 * HA + other * HB, HB), :].astype(BF)
    pl.semaphore_wait(barrier, Y + Z - 2 + 1)

    swap = remote(sb, rb, core_sem.at[0], core_sem.at[1], sibling)
    swap.start()
    swap.wait_recv()
    chip[0:HA, :] = (g[rows(c * HA, HA), :] + rb[0:HA, :].astype(F32)).astype(BF)
    chip[HA : HA + HB, :] = (g[rows(2 * HA + c * HB, HB), :] + rb[HA : HA + HB, :].astype(F32)).astype(BF)

    def a1(to, slot):
        return remote(chip.at[rows(to * PA, PA)], ra.at[slot], a1s.at[to], a1r.at[slot], at_y(to))

    def b1(to, slot):
        return remote(chip.at[rows(HA + to * PB, PB)], rbz.at[slot], b1s.at[to], b1r.at[slot], at_z(to))

    def first(i):
        a1(y_of(i), y).start()
        b1(z_of(i), z).start()

    each(Y, first)
    ra[y] = chip[rows(y * PA, PA), :]
    rbz[z] = chip[rows(HA + z * PB, PB), :]

    def total(ref):
        value = ref[0].astype(F32)
        for i in range(1, 8):
            value = value + ref[i].astype(F32)
        return value.astype(BF)

    each(Y, lambda i: a1(y_of(i), y_of(i)).wait_recv())
    ra2[z] = total(ra)

    def a2(to, slot):
        return remote(ra2.at[slot], ra2.at[slot], a2s.at[to], a2r.at[slot], at_z(to))

    each(Z, lambda i: a2(z_of(i), z).start())
    each(Z, lambda i: b1(z_of(i), z_of(i)).wait_recv())
    rb2[y] = total(rbz)

    def b2(to, slot):
        return remote(rb2.at[slot], rb2.at[slot], b2s.at[to], b2r.at[slot], at_y(to))

    each(Y, lambda i: b2(y_of(i), y).start())

    def a3(to, slot):
        ref = fin.at[rows(c * HA + slot * PA, PA)]
        return remote(ref, ref, a3s.at[to], a3r.at[slot], at_y(to))

    def b3(to, slot):
        ref = fin.at[rows(2 * HA + c * HB + slot * PB, PB)]
        return remote(ref, ref, b3s.at[to], b3r.at[slot], at_z(to))

    each(Z, lambda i: a2(z_of(i), z_of(i)).wait_recv())
    fin[rows(c * HA + y * PA, PA), :] = total(ra2)
    each(Y, lambda i: a3(y_of(i), y).start())
    each(Y, lambda i: b2(y_of(i), y_of(i)).wait_recv())
    fin[rows(2 * HA + c * HB + z * PB, PB), :] = total(rb2)
    each(Z, lambda i: b3(z_of(i), z).start())
    each(Y, lambda i: a3(y_of(i), y_of(i)).wait_recv())

    def end_a(core):
        ref = fin.at[rows(core * HA, HA)]
        return remote(ref, ref, end_sem.at[0], end_sem.at[1], sibling)

    def end_b(core):
        ref = fin.at[rows(2 * HA + core * HB, HB)]
        return remote(ref, ref, end_sem.at[2], end_sem.at[3], sibling)

    end_a(c).start()
    each(Z, lambda i: b3(z_of(i), z_of(i)).wait_recv())
    end_b(c).start()
    end_a(other).wait_recv()
    end_b(other).wait_recv()

    for k in range(4):
        ref = conv_out.at[0, k] if k < 3 else out_out.at[0]
        ref[:, 0:128] = fin[2 * k * C : (2 * k + 1) * C, :].astype(F32) * scale
        ref[:, 128:256] = fin[(2 * k + 1) * C : (2 * k + 2) * C, :].astype(F32) * scale
        tail = fin[(8 + k // 2) * C : (9 + k // 2) * C, :].astype(F32) * scale
        ref[:, 256:320] = tail[:, 64 * (k % 2) : 64 * (k % 2) + 64]

    swap.wait_send()

    def drained(i):
        a1(y_of(i), y).wait_send()
        b1(z_of(i), z).wait_send()
        a2(z_of(i), z).wait_send()
        b2(y_of(i), y).wait_send()
        a3(y_of(i), y).wait_send()
        b3(z_of(i), z).wait_send()

    each(Y, drained)
    end_a(c).wait_send()
    end_b(c).wait_send()


def embed(times, channels):
    half = channels // 2
    index = jnp.arange(half).astype(jnp.float32)
    freq = jnp.exp(index * (-math.log(10000.0) / half))
    angle = times.astype(jnp.float32)[..., None] * freq
    return jnp.concatenate([jnp.sin(angle), jnp.cos(angle)], -1)


def body(video, cotangent, timesteps, conv_weight, out_weight):
    emb = embed(timesteps[:, 0], C)
    anywhere = pl.BlockSpec(memory_space=pl.ANY)
    vmem = pl.BlockSpec(memory_space=pltpu.VMEM)
    dma = pltpu.SemaphoreType.DMA
    stack = (SECTIONS, ROWS, C)
    partial = pl.pallas_call(
        chain_kernel,
        out_shape=jax.ShapeDtypeStruct((TOTAL, 128), F32),
        in_specs=[anywhere, anywhere, vmem, anywhere, anywhere],
        out_specs=vmem,
        scratch_shapes=[
            pltpu.VMEM((2, 64, C), BF),
            pltpu.VMEM((2, 64, C), BF),
            pltpu.VMEM((SECTIONS, 4, C, C), BF),
            pltpu.VMEM((Z, 32, C), BF),
            pltpu.VMEM((Z, 32, C), BF),
            pltpu.VMEM((YL, 64, C), BF),
            pltpu.VMEM((YL, 64, C), BF),
            pltpu.VMEM(stack, BF),
            pltpu.VMEM(stack, BF),
            pltpu.VMEM(stack, F32),
            pltpu.VMEM(stack, BF),
            pltpu.VMEM(stack, BF),
            pltpu.VMEM(stack, BF),
            pltpu.VMEM(stack, BF),
            pltpu.VMEM(stack, BF),
            pltpu.VMEM(stack, BF),
            pltpu.VMEM(stack, BF),
            dma((4,)),
            dma((Z,)), dma((Z,)), dma((YL,)), dma((YL,)),
            dma((2, 2)), dma((SECTIONS, 2)), dma((2,)), dma((2,)),
            dma((SECTIONS,)), dma((SECTIONS,)), dma((SECTIONS, 4)), dma((SECTIONS, 4)),
            dma((SECTIONS,)), dma((SECTIONS,)), dma((SECTIONS,)), dma((SECTIONS,)),
        ],
        compiler_params=pltpu.CompilerParams(
            collective_id=1, has_side_effects=True, vmem_limit_bytes=48 << 20
        ),
        name="chain",
    )(video, cotangent, emb, conv_weight, out_weight)
    rows = video.shape[0] * 4 * 64 * video.shape[3]
    return pl.pallas_call(
        functools.partial(sum_kernel, 1.0 / math.sqrt(rows)),
        out_shape=(
            jax.ShapeDtypeStruct((1, 3, C, C), F32),
            jax.ShapeDtypeStruct((1, C, C), F32),
        ),
        in_specs=[vmem],
        out_specs=(vmem, vmem),
        scratch_shapes=[
            pltpu.VMEM((HA + HB, 128), BF),
            pltpu.VMEM((HA + HB, 128), BF),
            pltpu.VMEM((HA + HB, 128), BF),
            pltpu.VMEM((8, PA, 128), BF),
            pltpu.VMEM((8, PB, 128), BF),
            pltpu.VMEM((8, PA, 128), BF),
            pltpu.VMEM((8, PB, 128), BF),
            pltpu.VMEM((TOTAL, 128), BF),
            dma((2,)),
        ]
        + [dma((8,))] * 12
        + [dma((4,))],
        compiler_params=pltpu.CompilerParams(
            collective_id=2, has_side_effects=True, vmem_limit_bytes=48 << 20
        ),
        name="sum",
    )(partial)


def solution(mesh):
    return jax.shard_map(
        body,
        mesh=mesh,
        in_specs=(
            P(None, "dp", "tm", None, None),
            P(None, "dp", "tm", None, None),
            P(None, "dp"),
            P("pipe", None, None, None),
            P("pipe", None, None),
        ),
        out_specs=(P("pipe", None, None, None), P("pipe", None, None)),
        check_vma=False,
    )
```

time: 1160 us -> 89.4 us (0.08)
  blocking collectives: 670 us -> 0 us
  waiting for transfers between devices: 325 us -> 0 us
  starting transfers between devices: 111 us -> 0 us
  Pallas kernels: 0 us -> 81.3 us
  matrix products: 18.2 us -> 0 us
  between operations: 15.5 us -> 0.66 us
  other arithmetic: 13.4 us -> 0.86 us
    psum x1 -> x0, blocking collectives: 670 us -> none  [body(): down_sum, up_sum = lax.psum((down_total, up_total), ('tm', 'dp'))]
    psum x1 -> x0, waiting for transfers between devices: 213 us -> none  [body(): down_sum, up_sum = lax.psum((down_total, up_total), ('tm', 'dp'))]
    ppermute x38 -> x0, waiting for transfers between devices: 112 us -> none  [the longest x4 55.5 us: from_partner(): return lax.ppermute(value, axis, pairs)]
    ppermute x38 -> x0, starting transfers between devices: 111 us -> none  [the longest x9 39.3 us: padded_2(): lax.ppermute(lax.slice_in_dim(block, block.shape[dim] - width, None, axis...]
    pallas_call x0 -> x2, Pallas kernels: none -> 81.3 us  [the longest x1 47.7 us: body(): pl.pallas_call(chain_kernel, out_shape=jax.ShapeDtypeStruct((TOTAL, 128),...]
    dot_general x56 -> x0, matrix products: 18.2 us -> none  [the longest x15 5.05 us: body(): jnp.einsum('dfpc,dfpx->dcx', padded[:, offset:offset + frames], grad_pre,...]
  transfers between devices with their start and end apart: 39 -> 0, of which waited for: 29 -> 0; matrix products, arithmetic and copies ran while one was open for 1% -> 0% of each run, Pallas kernels for 0% -> 0%
where the time goes in v1:
time: 89.4 us; the launch traced here: 88.7 us
  Pallas kernels  81.3 us (91%)
  local copies, waits for them, and re-layouts  5.94 us (7%)
    pallas_call x1, Pallas kernels, body(): pl.pallas_call(chain_kernel, out_shape=jax.ShapeDtypeStruct((TOTAL, 128),...  47.7 us
    pallas_call x1, Pallas kernels, body(): pl.pallas_call(functools.partial(sum_kernel, 1.0 / math.sqrt(rows)), out_...  33.6 us
    unnamed x10, local copies, waits for them, and re-layouts  5.94 us

profile of v1, /device:TPU:1, one launch (start us, length us, event | category | flops | bytes accessed | tf_op | source)
XLA Modules:
  0.0 88.7 jit_solution(12927905707886142520)
XLA Ops:
  0.6 0.7 convert_bitcast_fusion
  1.3 0.1 multiply_sine_fusion
  1.4 0.1 pad_maximum_fusion.emb
  1.5 0.0 copy-start
  1.5 1.1 %copy-done = bf16[1,3,320,320]{3,2,1,0:T(8,128)(2,1)S(1)} copy-done((bf16[1,3,320,320]{3,2,1,0:T(8,128)(2,1)S(1)}, bf16[1,3,320,320]{3,2,1,0:T(8,128)(2,1)}, u32[]{:S(2)}) %copy-start) | copy-done | bytes 614424
  2.6 0.0 copy-start.1
  2.6 1.0 %copy-done.1 = bf16[4,1,2,64,320]{4,3,2,1,0:T(8,128)(2,1)S(1)} copy-done((bf16[4,1,2,64,320]{4,3,2,1,0:T(8,128)(2,1)S(1)}, bf16[4,1,2,64,320]{4,3,2,1,0:T(8,128)(2,1)}, u32[]{:S(2)}) %copy-start.1) | copy-done | bytes 327704
  3.6 0.0 copy-start.2
  3.6 1.0 %copy-done.2 = bf16[4,1,2,64,320]{4,3,2,1,0:T(8,128)(2,1)S(1)} copy-done((bf16[4,1,2,64,320]{4,3,2,1,0:T(8,128)(2,1)S(1)}, bf16[4,1,2,64,320]{4,3,2,1,0:T(8,128)(2,1)}, u32[]{:S(2)}) %copy-start.2) | copy-done | bytes 327704
  4.6 0.0 copy-start.3
  4.6 0.9 %copy-done.3 = bf16[1,320,320]{2,1,0:T(8,128)(2,1)S(1)} copy-done((bf16[1,320,320]{2,1,0:T(8,128)(2,1)S(1)}, bf16[1,320,320]{2,1,0:T(8,128)(2,1)}, u32[]{:S(2)}) %copy-start.3) | copy-done | bytes 204824
  5.6 47.7 %chain.1.g = f32[3328,128]{1,0:T(8,128)S(1)} custom-call(bf16[4,1,2,64,320]{4,3,2,1,0:T(8,128)(2,1)S(1)} %copy-done.1, bf16[4,1,2,64,320]{4,3,2,1,0:T(8,128)(2,1)S(1)} %copy-done.2, f32[4,320]{1,0:T(4,128)S(1)} %pad_maximum_fusion.emb, bf16[1,3,320,320]{3,2,1,0:T(8,128)(2,1)S(1)} %copy-done, bf16[1,320,320]{2,1,0:T(8,128)(2,1)S(1)} %copy-done.3), custom_call_target="tpu_custom_call" | custom-call | tf_op jit(solution)/shard_map/chain/pallas_call | solution.py:448
  53.2 33.6 %sum.1 = (f32[1,3,320,320]{3,2,1,0:T(8,128)S(1)}, f32[1,320,320]{2,1,0:T(8,128)S(1)}) custom-call(f32[3328,128]{1,0:T(8,128)S(1)} %chain.1.g), custom_call_target="tpu_custom_call" | custom-call | tf_op jit(solution)/shard_map/sum/pallas_call | solution.py:483
  86.8 1.1 %copy.9 = f32[1,3,320,320]{3,2,1,0:T(8,128)} copy(f32[1,3,320,320]{3,2,1,0:T(8,128)S(1)} %get-tuple-element.6) | data formatting | bytes 2457600
  87.9 0.8 copy.10
  (1 shorter events, 0.0 us)
Async XLA Ops:
  1.5 1.1 %copy-start = (bf16[1,3,320,320]{3,2,1,0:T(8,128)(2,1)S(1)}, bf16[1,3,320,320]{3,2,1,0:T(8,128)(2,1)}, u32[]{:S(2)}) copy-start(bf16[1,3,320,320]{3,2,1,0:T(8,128)(2,1)} %convw.1) | copy-start | bytes 1843204
  2.6 1.0 %copy-start.1 = (bf16[4,1,2,64,320]{4,3,2,1,0:T(8,128)(2,1)S(1)}, bf16[4,1,2,64,320]{4,3,2,1,0:T(8,128)(2,1)}, u32[]{:S(2)}) copy-start(bf16[4,1,2,64,320]{4,3,2,1,0:T(8,128)(2,1)} %video.1) | copy-start | bytes 983044
  3.6 1.0 %copy-start.2 = (bf16[4,1,2,64,320]{4,3,2,1,0:T(8,128)(2,1)S(1)}, bf16[4,1,2,64,320]{4,3,2,1,0:T(8,128)(2,1)}, u32[]{:S(2)}) copy-start(bf16[4,1,2,64,320]{4,3,2,1,0:T(8,128)(2,1)} %cotangent.1) | copy-start | bytes 983044
  4.6 0.9 %copy-start.3 = (bf16[1,320,320]{2,1,0:T(8,128)(2,1)S(1)}, bf16[1,320,320]{2,1,0:T(8,128)(2,1)}, u32[]{:S(2)}) copy-start(bf16[1,320,320]{2,1,0:T(8,128)(2,1)} %outw.1) | copy-start | bytes 614404

commit v2 on v1

v2 whole, which is shorter than its diff:
```python
import functools
import math

import jax
import jax.numpy as jnp
from jax import lax
from jax.experimental import pallas as pl
from jax.experimental.pallas import tpu as pltpu
from jax.sharding import PartitionSpec as P

EPSILON = 1e-06
MESH = pl.DeviceIdType.MESH
SECTIONS = 4
C = 320
ROWS = 128
YL, Z, Y = 4, 8, 8
PA, PB = 112, 96
HA, HB = 8 * PA, 8 * PB
HALF = HA + HB
CHUNK_A, CHUNK_B = ((0, 64), (64, 48)), ((0, 48), (48, 48))
QUARTER = C // 2
BF = jnp.bfloat16
F32 = jnp.float32


def place():
    p, t, d = lax.axis_index("pipe"), lax.axis_index("tm"), lax.axis_index("dp")
    return p, lax.div(d, 2) * YL + lax.div(t, Z), lax.rem(t, Z), lax.rem(d, 2)


def device(p, y, z, c):
    return (p, lax.rem(y, YL) * Z + z, lax.div(y, YL) * 2 + c)


def remote(src, dst, send, recv, to):
    return pltpu.make_async_remote_copy(
        src_ref=src, dst_ref=dst, send_sem=send, recv_sem=recv, device_id=to, device_id_type=MESH
    )


def each(count, fn):
    def step(i, _):
        fn(i)
        return 0

    lax.fori_loop(1, count, step, 0)


def dot(a, b):
    return jnp.dot(a, b, preferred_element_type=F32)


def dot_t(a, b):
    return lax.dot_general(a, b, (((1,), (1,)), ((), ())), preferred_element_type=F32)


def t_dot(a, b):
    return lax.dot_general(a, b, (((0,), (0,)), ((), ())), preferred_element_type=F32)


def normalize(h):
    x = h.astype(F32)
    inv = lax.rsqrt(jnp.mean(x * x, -1, keepdims=True) + EPSILON)
    return x, inv, x * inv


def before(v):
    row = lax.rem(lax.broadcasted_iota(jnp.int32, v.shape, 0), ROWS)
    return jnp.where(row < 2, 0.0, pltpu.roll(v, 2, 0))


def after(v):
    row = lax.rem(lax.broadcasted_iota(jnp.int32, v.shape, 0), ROWS)
    return jnp.where(row >= ROWS - 2, 0.0, pltpu.roll(v, v.shape[0] - 2, 0))


def reorder(source_of, v):
    r = lax.broadcasted_iota(jnp.int32, (ROWS, ROWS), 0)
    k = lax.broadcasted_iota(jnp.int32, (ROWS, ROWS), 1)
    pick = jnp.where(source_of(r) == k, 1.0, 0.0).astype(BF)
    return dot(pick, v).astype(BF)


def to_z(r):
    return lax.rem(lax.div(r, 8), 2) * 64 + lax.div(r, 16) * 8 + lax.rem(r, 8)


def to_y(r):
    return lax.div(lax.rem(r, 32), 2) * 8 + lax.div(r, 32) * 2 + lax.rem(r, 2)


def kernel(
    video, cotangent, times, convw, outw, fin,
    vin, cin, tin, emb, w, s1s, s1d, s2s, s2d, hs, ds, pre_s, hr, lhs, rhs,
    gown, sb, rb, chip, ra, rbz, ra2, rb2,
    in_sem, z_send, z_recv, y_send, y_recv,
    x_send, x_recv, n_send, n_recv, c_send, c_recv,
    h_send, h_recv, d_send, d_recv,
    core_sem, a1s, a1r, b1s, b1r, a2s, a2r, b2s, b2r, a3s, a3r, b3s, b3r, end_sem,
):
    p, y, z, c = place()
    yl = lax.rem(y, YL)
    ybase = y - yl
    other = 1 - c
    loads = [
        pltpu.make_async_copy(convw.at[0], w.at[p, pl.ds(0, 6)], in_sem.at[2]),
        pltpu.make_async_copy(outw.at[0], w.at[p, pl.ds(6, 2)], in_sem.at[3]),
        pltpu.make_async_copy(video.at[p, 0], vin, in_sem.at[0]),
        pltpu.make_async_copy(cotangent.at[p, 0], cin, in_sem.at[1]),
        pltpu.make_async_copy(times, tin, in_sem.at[4]),
    ]
    for load in loads:
        load.start()

    barrier = pltpu.get_barrier_semaphore()

    def greet(to):
        pl.semaphore_signal(barrier, inc=1, device_id=to, device_id_type=MESH)

    def at_x(to):
        return device(to, y, z, c)

    def at_y(to):
        return device(p, to, z, c)

    def at_z(to):
        return device(p, y, to, c)

    def x_of(i):
        return lax.rem(p + i, SECTIONS)

    def y_of(i):
        return lax.rem(y + i, Y)

    def z_of(i):
        return lax.rem(z + i, Z)

    sibling = device(p, y, z, other)
    each(SECTIONS, lambda i: greet(at_x(x_of(i))))
    each(Y, lambda i: greet(at_y(y_of(i))))
    each(Z, lambda i: greet(at_z(z_of(i))))
    greet(sibling)
    for load in loads:
        load.wait()
    pl.semaphore_wait(barrier, SECTIONS + Y + Z - 3 + 1)

    color = lax.rem((y + 2 * z) * other + (2 * y + z) * c, 4)
    step_y, step_z = other, c
    nexts = [
        device(p, lax.rem(y + step_y, Y), lax.rem(z + step_z, Z), c),
        device(p, lax.rem(y + Y - step_y, Y), lax.rem(z + Z - step_z, Z), c),
        device(p, lax.rem(y + step_z, Y), lax.rem(z + step_y, Z), c),
        device(p, lax.rem(y + Y - step_z, Y), lax.rem(z + Z - step_y, Z), c),
    ]
    parts = [pl.ds(0, QUARTER), pl.ds(0, QUARTER), pl.ds(0, QUARTER // 2), pl.ds(QUARTER // 2, QUARTER // 2)]
    quarter = [lax.rem(color + k, 4) for k in range(4)]

    def over_x(section, to):
        ref = w.at[section, 4 * c + color]
        return remote(ref, ref, x_send.at[to], x_recv.at[section], at_x(to))

    def to_next(section, way, part):
        ref = w.at[section, 4 * c + part, parts[way]]
        return remote(ref, ref, n_send.at[section, way], n_recv.at[section, way], nexts[way])

    def to_core(section, core, part):
        ref = w.at[section, 4 * core + part]
        return remote(ref, ref, c_send.at[section, part], c_recv.at[section, part], sibling)

    right, left, far = x_of(1), x_of(3), x_of(2)
    for to in (right, left, far):
        over_x(p, to).start()

    s1s[:, 0:16, :] = reorder(to_z, vin[...].reshape(ROWS, C)).reshape(Z, 16, C)
    s1s[:, 16:32, :] = reorder(to_z, cin[...].reshape(ROWS, C)).reshape(Z, 16, C)

    def z_copy(at, slot):
        return remote(s1s.at[at], s1d.at[slot], z_send.at[at], z_recv.at[slot], at_z(at))

    each(Z, lambda i: z_copy(z_of(i), z).start())
    s1d[z] = s1s[z]

    lane = lax.broadcasted_iota(jnp.int32, (1, C), 1)
    index = jnp.where(lane < C // 2, lane, lane - C // 2).astype(F32)
    freq = jnp.exp(index * (-math.log(10000.0) / (C // 2)))
    for m in range(SECTIONS):
        angle = tin[:, m : m + 1].astype(F32) * freq
        emb[m : m + 1, :] = jnp.where(lane < C // 2, jnp.sin(angle), jnp.cos(angle))

    def spread(section):
        over_x(section, p).wait_recv()
        for way in range(4):
            to_next(section, way, color).start()
        to_core(section, c, color).start()

    spread(left)
    spread(right)

    each(Z, lambda i: z_copy(z_of(i), z_of(i)).wait_recv())
    for kind in range(2):
        s2s[kind] = reorder(to_y, s1d[:, 16 * kind : 16 * kind + 16, :].reshape(ROWS, C)).reshape(YL, 32, C)

    def yl_of(i):
        return lax.rem(yl + i, YL)

    def y_copy(kind, at, slot):
        return remote(
            s2s.at[kind, at], s2d.at[kind, slot], y_send.at[kind, at], y_recv.at[kind, slot], at_y(ybase + at)
        )

    each(YL, lambda i: y_copy(0, yl_of(i), yl).start())
    spread(far)
    each(YL, lambda i: y_copy(1, yl_of(i), yl).start())
    s2d[0, yl] = s2s[0, yl]
    s2d[1, yl] = s2s[1, yl]

    def give(value, kept, send, recv, section):
        copy = remote(value.at[section], kept.at[p], send.at[section], recv.at[p], at_x(section))

        @pl.when(p != section)
        def _():
            copy.start()

        @pl.when(p == section)
        def _():
            kept[p] = value[section]

    dr = rhs.at[3]
    each(YL, lambda i: y_copy(0, yl_of(i), yl_of(i)).wait_recv())
    hs[0] = s2d[0].reshape(ROWS, C)
    give(hs, hr, h_send, h_recv, 0)

    for section in (left, right, far):
        to_next(section, 0, quarter[3]).wait_recv()
        to_core(section, c, quarter[3]).start()
        to_next(section, 1, quarter[1]).wait_recv()
        to_core(section, c, quarter[1]).start()
        to_next(section, 2, quarter[2]).wait_recv()
        to_next(section, 3, quarter[2]).wait_recv()
        to_core(section, c, quarter[2]).start()

    each(YL, lambda i: y_copy(1, yl_of(i), yl_of(i)).wait_recv())
    ds[3] = s2d[1].reshape(ROWS, C)
    give(ds, dr, d_send, d_recv, 3)

    for section in (left, right, far):
        for part in range(4):
            to_core(section, other, part).wait_recv()

    def weight(section, k):
        return w[section, 2 * k : 2 * k + 2].reshape(C, C)

    emb_row = emb[pl.ds(p, 1), :]
    for s in range(SECTIONS):
        x, inv, normed = normalize(hs[s])
        pre = emb_row + dot(before(normed).astype(BF), weight(s, 0))
        pre = pre + dot(normed.astype(BF), weight(s, 1))
        pre = pre + dot(after(normed).astype(BF), weight(s, 2))
        pre_s[s] = pre
        if s + 1 < SECTIONS:
            act = (pre * jax.nn.sigmoid(pre)).astype(BF)
            hs[s + 1] = (x + dot(act, weight(s, 3))).astype(BF)
            give(hs, hr, h_send, h_recv, s + 1)
    for s in (3, 2, 1):
        x, inv, normed = normalize(hs[s])
        grad = ds[s]
        pre = pre_s[s]
        sig = jax.nn.sigmoid(pre)
        dpre = dot_t(grad, weight(s, 3)) * sig * (1.0 + pre * (1.0 - sig))
        dnorm = dot_t(after(dpre).astype(BF), weight(s, 0))
        dnorm = dnorm + dot_t(dpre.astype(BF), weight(s, 1))
        dnorm = dnorm + dot_t(before(dpre).astype(BF), weight(s, 2))
        mean = jnp.mean(dnorm * normed, -1, keepdims=True)
        ds[s - 1] = (grad.astype(F32) + inv * (dnorm - normed * mean)).astype(BF)
        give(ds, dr, d_send, d_recv, s - 1)

    def take(kept, value, send, recv):
        def one(i):
            m = x_of(i)
            remote(value.at[0], kept.at[m], send.at[0], recv.at[m], at_x(m)).wait_recv()

        each(SECTIONS, one)

    take(hr, hs, h_send, h_recv)

    def redo(m, _):
        x, inv, normed = normalize(hr[m])
        low = normed.astype(BF)
        pre = emb[pl.ds(m, 1), :] + dot(before(normed).astype(BF), weight(p, 0))
        pre = pre + dot(low, weight(p, 1))
        pre = pre + dot(after(normed).astype(BF), weight(p, 2))
        pre_s[m] = pre
        lhs[0, m] = low
        lhs[1, m] = (pre * jax.nn.sigmoid(pre)).astype(BF)
        return 0

    lax.fori_loop(0, SECTIONS, redo, 0)
    take(dr, ds, d_send, d_recv)

    def redo_back(m, _):
        pre = pre_s[m]
        sig = jax.nn.sigmoid(pre)
        dpre = dot_t(rhs[3, m], weight(p, 3)) * sig * (1.0 + pre * (1.0 - sig))
        rhs[0, m] = after(dpre).astype(BF)
        rhs[1, m] = dpre.astype(BF)
        rhs[2, m] = before(dpre).astype(BF)
        return 0

    lax.fori_loop(0, SECTIONS, redo_back, 0)

    def gradients(core, ref):
        tails = []
        for j in range(2):
            k = 2 * core + j
            term = t_dot(
                lhs[lax.div(k, 3)].reshape(SECTIONS * ROWS, C), rhs[k].reshape(SECTIONS * ROWS, C)
            )
            ref[2 * j * C : (2 * j + 1) * C, :] = term[:, 0:128].astype(ref.dtype)
            ref[(2 * j + 1) * C : (2 * j + 2) * C, :] = term[:, 128:256].astype(ref.dtype)
            tails.append(term[:, 256:320])
        ref[4 * C : 5 * C, :] = jnp.concatenate(tails, 1).astype(ref.dtype)
        ref[5 * C : HALF, :] = jnp.zeros((HALF - 5 * C, 128), ref.dtype)

    gradients(other, sb)
    swap = remote(sb, rb, core_sem.at[0], core_sem.at[1], sibling)
    swap.start()
    gradients(c, gown)
    swap.wait_recv()
    chip[...] = (gown[...] + rb[...].astype(F32)).astype(BF)

    def rows(start, size):
        return pl.ds(pl.multiple_of(start, 16), size)

    def a1(q, to, slot):
        lo, n = CHUNK_A[q]
        return remote(
            chip.at[rows(to * PA + lo, n)], ra.at[slot, pl.ds(lo, n)], a1s.at[q, to], a1r.at[q, slot], at_y(to)
        )

    def b1(q, to, slot):
        lo, n = CHUNK_B[q]
        return remote(
            chip.at[rows(HA + to * PB + lo, n)], rbz.at[slot, pl.ds(lo, n)], b1s.at[q, to], b1r.at[q, slot], at_z(to)
        )

    def a2(q, to, slot):
        ref = ra2.at[slot, pl.ds(*CHUNK_A[q])]
        return remote(ref, ref, a2s.at[q, to], a2r.at[q, slot], at_z(to))

    def b2(q, to, slot):
        ref = rb2.at[slot, pl.ds(*CHUNK_B[q])]
        return remote(ref, ref, b2s.at[q, to], b2r.at[q, slot], at_y(to))

    def a3(q, to, slot):
        lo, n = CHUNK_A[q]
        ref = fin.at[c, rows(slot * PA + lo, n)]
        return remote(ref, ref, a3s.at[q, to], a3r.at[q, slot], at_y(to))

    def b3(q, to, slot):
        lo, n = CHUNK_B[q]
        ref = fin.at[c, rows(HA + slot * PB + lo, n)]
        return remote(ref, ref, b3s.at[q, to], b3r.at[q, slot], at_z(to))

    def total(ref, chunk):
        lo, n = chunk
        value = ref[0, lo : lo + n].astype(F32)
        for i in range(1, 8):
            value = value + ref[i, lo : lo + n].astype(F32)
        return value.astype(BF)

    for q in range(2):

        def first(i):
            a1(q, y_of(i), y).start()
            b1(q, z_of(i), z).start()

        each(Y, first)
    ra[y] = chip[rows(y * PA, PA), :]
    rbz[z] = chip[rows(HA + z * PB, PB), :]
    for q in range(2):
        lo, n = CHUNK_A[q]
        each(Y, lambda i: a1(q, y_of(i), y_of(i)).wait_recv())
        ra2[z, lo : lo + n] = total(ra, (lo, n))
        each(Z, lambda i: a2(q, z_of(i), z).start())
        lo, n = CHUNK_B[q]
        each(Z, lambda i: b1(q, z_of(i), z_of(i)).wait_recv())
        rb2[y, lo : lo + n] = total(rbz, (lo, n))
        each(Y, lambda i: b2(q, y_of(i), y).start())
    for q in range(2):
        lo, n = CHUNK_A[q]
        each(Z, lambda i: a2(q, z_of(i), z_of(i)).wait_recv())
        fin[c, rows(y * PA + lo, n), :] = total(ra2, (lo, n))
        each(Y, lambda i: a3(q, y_of(i), y).start())
        lo, n = CHUNK_B[q]
        each(Y, lambda i: b2(q, y_of(i), y_of(i)).wait_recv())
        fin[c, rows(HA + z * PB + lo, n), :] = total(rb2, (lo, n))
        each(Z, lambda i: b3(q, z_of(i), z).start())

    def end(core, which):
        ref = fin.at[core, pl.ds(HA * which, HB if which else HA)]
        return remote(ref, ref, end_sem.at[0, which], end_sem.at[1, which], sibling)

    for q in range(2):
        each(Y, lambda i: a3(q, y_of(i), y_of(i)).wait_recv())
    end(c, 0).start()
    for q in range(2):
        each(Z, lambda i: b3(q, z_of(i), z_of(i)).wait_recv())
    end(c, 1).start()
    end(other, 0).wait_recv()
    end(other, 1).wait_recv()

    for to in (right, left, far):
        over_x(p, to).wait_send()
    for section in (left, right, far):
        for way in range(4):
            to_next(section, way, color).wait_send()
        for part in range(4):
            to_core(section, c, part).wait_send()
    each(Z, lambda i: z_copy(z_of(i), z).wait_send())
    for kind in range(2):
        each(YL, lambda i: y_copy(kind, yl_of(i), yl).wait_send())

    def left_us(i):
        s = x_of(i)
        remote(hs.at[s], hr.at[p], h_send.at[s], h_recv.at[p], at_x(s)).wait_send()
        remote(ds.at[s], dr.at[p], d_send.at[s], d_recv.at[p], at_x(s)).wait_send()

    each(SECTIONS, left_us)
    swap.wait_send()
    for q in range(2):

        def drained(i):
            a1(q, y_of(i), y).wait_send()
            b1(q, z_of(i), z).wait_send()
            a2(q, z_of(i), z).wait_send()
            b2(q, y_of(i), y).wait_send()
            a3(q, y_of(i), y).wait_send()
            b3(q, z_of(i), z).wait_send()

        each(Y, drained)
    end(c, 0).wait_send()
    end(c, 1).wait_send()


def unpack_kernel(scale, fin, conv_out, out_out):
    for k in range(4):
        ref = conv_out.at[0, k] if k < 3 else out_out.at[0]
        core, j = divmod(k, 2)
        ref[:, 0:128] = fin[core, 2 * j * C : (2 * j + 1) * C, :].astype(F32) * scale
        ref[:, 128:256] = fin[core, (2 * j + 1) * C : (2 * j + 2) * C, :].astype(F32) * scale
        tail = fin[core, 4 * C : 5 * C, :].astype(F32) * scale
        ref[:, 256:320] = tail[:, 64 * j : 64 * j + 64]


def body(video, cotangent, timesteps, conv_weight, out_weight):
    far_memory = pl.BlockSpec(memory_space=pltpu.HBM)
    vmem = pl.BlockSpec(memory_space=pltpu.VMEM)
    dma = pltpu.SemaphoreType.DMA
    stack = (SECTIONS, ROWS, C)
    rows = video.shape[0] * 4 * 64 * video.shape[3]
    packed = pl.pallas_call(
        kernel,
        out_shape=jax.ShapeDtypeStruct((2, HALF, 128), BF),
        in_specs=[far_memory] * 5,
        out_specs=vmem,
        scratch_shapes=[
            pltpu.VMEM((2, 64, C), BF),
            pltpu.VMEM((2, 64, C), BF),
            pltpu.VMEM((1, SECTIONS), jnp.int32),
            pltpu.VMEM((SECTIONS, C), F32),
            pltpu.VMEM((SECTIONS, 8, QUARTER, C), BF),
            pltpu.VMEM((Z, 32, C), BF),
            pltpu.VMEM((Z, 32, C), BF),
            pltpu.VMEM((2, YL, 32, C), BF),
            pltpu.VMEM((2, YL, 32, C), BF),
            pltpu.VMEM(stack, BF),
            pltpu.VMEM(stack, BF),
            pltpu.VMEM(stack, F32),
            pltpu.VMEM(stack, BF),
            pltpu.VMEM((2, *stack), BF),
            pltpu.VMEM((4, *stack), BF),
            pltpu.VMEM((HALF, 128), F32),
            pltpu.VMEM((HALF, 128), BF),
            pltpu.VMEM((HALF, 128), BF),
            pltpu.VMEM((HALF, 128), BF),
            pltpu.VMEM((8, PA, 128), BF),
            pltpu.VMEM((8, PB, 128), BF),
            pltpu.VMEM((8, PA, 128), BF),
            pltpu.VMEM((8, PB, 128), BF),
            dma((5,)),
            dma((Z,)), dma((Z,)), dma((2, YL)), dma((2, YL)),
            dma((SECTIONS,)), dma((SECTIONS,)),
            dma((SECTIONS, 4)), dma((SECTIONS, 4)), dma((SECTIONS, 4)), dma((SECTIONS, 4)),
            dma((SECTIONS,)), dma((SECTIONS,)), dma((SECTIONS,)), dma((SECTIONS,)),
            dma((2,)),
        ]
        + [dma((2, 8))] * 12
        + [dma((2, 2))],
        compiler_params=pltpu.CompilerParams(
            collective_id=1, has_side_effects=True, vmem_limit_bytes=56 << 20
        ),
        name="main",
    )(
        video,
        cotangent,
        timesteps.T,
        conv_weight.reshape(1, 6, QUARTER, C),
        out_weight.reshape(1, 2, QUARTER, C),
    )
    return pl.pallas_call(
        functools.partial(unpack_kernel, 1.0 / math.sqrt(rows)),
        out_shape=(
            jax.ShapeDtypeStruct((1, 3, C, C), F32),
            jax.ShapeDtypeStruct((1, C, C), F32),
        ),
        in_specs=[vmem],
        out_specs=(vmem, vmem),
        name="unpack",
    )(packed)


def solution(mesh):
    return jax.shard_map(
        body,
        mesh=mesh,
        in_specs=(
            P(None, "dp", "tm", None, None),
            P(None, "dp", "tm", None, None),
            P(None, "dp"),
            P("pipe", None, None, None),
            P("pipe", None, None),
        ),
        out_specs=(P("pipe", None, None, None), P("pipe", None, None)),
        check_vma=False,
    )
```

time: 89.4 us -> 77.1 us (0.86)
  local copies, waits for them, and re-layouts: 5.94 us -> 0 us
  Pallas kernels: 81.3 us -> 76.2 us
    unnamed x10 -> x0, local copies, waits for them, and re-layouts: 5.94 us -> none
    pallas_call x2, Pallas kernels: 81.3 us -> 76.2 us  [the longest x1 73.6 us: body(): pl.pallas_call(kernel, out_shape=jax.ShapeDtypeStruct((2, HALF, 128), BF)...]
where the time goes in v2:
time: 77.1 us; the launch traced here: 76.9 us
  Pallas kernels  76.2 us (99%)
    pallas_call x1, Pallas kernels, body(): pl.pallas_call(kernel, out_shape=jax.ShapeDtypeStruct((2, HALF, 128), BF)...  73.6 us
    pallas_call x1, Pallas kernels, body(): pl.pallas_call(functools.partial(unpack_kernel, 1.0 / math.sqrt(rows)), o...  2.6 us

profile of v2, /device:TPU:1, one launch (start us, length us, event | category | flops | bytes accessed | tf_op | source)
XLA Modules:
  0.0 76.9 jit_solution(14293063331502044126)
XLA Ops:
  0.6 73.6 %main.1.fin = bf16[2,1664,128]{2,1,0:T(8,128)(2,1)} custom-call(bf16[4,1,2,64,320]{4,3,2,1,0:T(8,128)(2,1)} %video.1, bf16[4,1,2,64,320]{4,3,2,1,0:T(8,128)(2,1)} %cotangent.1, s32[1,4]{1,0:T(1,128)} %bitcast.5, bf16[1,6,160,320]{3,2,1,0:T(8,128)(2,1)} %bitcast.3, bf16[1,2,160,320]{3,2,1,0:T(8,128)(2,1)} %bitcast.4), custom_call_target="tpu_custom_call" | custom-call | tf_op jit(solution)/shard_map/main/pallas_call | solution.py:461
  74.3 2.6 %unpack.1 = (f32[1,3,320,320]{3,2,1,0:T(8,128)}, f32[1,320,320]{2,1,0:T(8,128)}) custom-call(bf16[2,1664,128]{2,1,0:T(8,128)(2,1)} %main.1.fin), custom_call_target="tpu_custom_call" | custom-call | tf_op jit(solution)/shard_map/unpack/pallas_call | solution.py:510

commit v3 on v2

--- a/solution.py
+++ b/solution.py
@@ -17,7 +17,8 @@
 PA, PB = 112, 96
 HA, HB = 8 * PA, 8 * PB
 HALF = HA + HB
-CHUNK_A, CHUNK_B = ((0, 64), (64, 48)), ((0, 48), (48, 48))
+CHUNK_A, CHUNK_B = ((0, 48), (48, 32), (80, 32)), ((0, 32), (32, 32), (64, 32))
+CHUNKS = 3
 QUARTER = C // 2
 BF = jnp.bfloat16
 F32 = jnp.float32
@@ -90,13 +91,13 @@
 
 
 def kernel(
-    video, cotangent, times, convw, outw, fin,
+    video, cotangent, times, convw, outw, packed,
     vin, cin, tin, emb, w, s1s, s1d, s2s, s2d, hs, ds, pre_s, hr, lhs, rhs,
-    gown, sb, rb, chip, ra, rbz, ra2, rb2,
+    gown, sb, rb, chip, ra, rbz, ra2, rb2, fin,
     in_sem, z_send, z_recv, y_send, y_recv,
     x_send, x_recv, n_send, n_recv, c_send, c_recv,
     h_send, h_recv, d_send, d_recv,
-    core_sem, a1s, a1r, b1s, b1r, a2s, a2r, b2s, b2r, a3s, a3r, b3s, b3r, end_sem,
+    core_sem, a1s, a1r, b1s, b1r, a2s, a2r, b2s, b2r, a3s, a3r, b3s, b3r, end_sem, out_sem,
 ):
     p, y, z, c = place()
     yl = lax.rem(y, YL)
@@ -168,7 +169,8 @@
         return remote(ref, ref, c_send.at[section, part], c_recv.at[section, part], sibling)
 
     right, left, far = x_of(1), x_of(3), x_of(2)
-    for to in (right, left, far):
+    first = p == 0
+    for to in (jnp.where(first, far, right), jnp.where(first, right, left), jnp.where(first, left, far)):
         over_x(p, to).start()
 
     s1s[:, 0:16, :] = reorder(to_z, vin[...].reshape(ROWS, C)).reshape(Z, 16, C)
@@ -187,18 +189,32 @@
         angle = tin[:, m : m + 1].astype(F32) * freq
         emb[m : m + 1, :] = jnp.where(lane < C // 2, jnp.sin(angle), jnp.cos(angle))
 
+    def unless_own(section, fn):
+        @pl.when(p != section)
+        def _():
+            fn(section)
+
     def spread(section):
         over_x(section, p).wait_recv()
         for way in range(4):
             to_next(section, way, color).start()
         to_core(section, c, color).start()
 
-    spread(left)
-    spread(right)
+    def relay(section):
+        for way, k in ((0, 3), (1, 1), (2, 2)):
+            to_next(section, way, quarter[k]).wait_recv()
+            if way == 2:
+                to_next(section, 3, quarter[k]).wait_recv()
+            to_core(section, c, quarter[k]).start()
+
+    def complete(section):
+        for part in range(4):
+            to_core(section, other, part).wait_recv()
+
+    unless_own(0, spread)
+    unless_own(1, spread)
 
     each(Z, lambda i: z_copy(z_of(i), z_of(i)).wait_recv())
-    for kind in range(2):
-        s2s[kind] = reorder(to_y, s1d[:, 16 * kind : 16 * kind + 16, :].reshape(ROWS, C)).reshape(YL, 32, C)
 
     def yl_of(i):
         return lax.rem(yl + i, YL)
@@ -208,11 +224,11 @@
             s2s.at[kind, at], s2d.at[kind, slot], y_send.at[kind, at], y_recv.at[kind, slot], at_y(ybase + at)
         )
 
-    each(YL, lambda i: y_copy(0, yl_of(i), yl).start())
-    spread(far)
-    each(YL, lambda i: y_copy(1, yl_of(i), yl).start())
-    s2d[0, yl] = s2s[0, yl]
-    s2d[1, yl] = s2s[1, yl]
+    for kind in range(2):
+        s2s[kind] = reorder(to_y, s1d[:, 16 * kind : 16 * kind + 16, :].reshape(ROWS, C)).reshape(YL, 32, C)
+        each(YL, lambda i: y_copy(kind, yl_of(i), yl).start())
+        unless_own(2 + kind, spread)
+        s2d[kind, yl] = s2s[kind, yl]
 
     def give(value, kept, send, recv, section):
         copy = remote(value.at[section], kept.at[p], send.at[section], recv.at[p], at_x(section))
@@ -226,32 +242,18 @@
             kept[p] = value[section]
 
     dr = rhs.at[3]
+    unless_own(0, relay)
     each(YL, lambda i: y_copy(0, yl_of(i), yl_of(i)).wait_recv())
     hs[0] = s2d[0].reshape(ROWS, C)
     give(hs, hr, h_send, h_recv, 0)
-
-    for section in (left, right, far):
-        to_next(section, 0, quarter[3]).wait_recv()
-        to_core(section, c, quarter[3]).start()
-        to_next(section, 1, quarter[1]).wait_recv()
-        to_core(section, c, quarter[1]).start()
-        to_next(section, 2, quarter[2]).wait_recv()
-        to_next(section, 3, quarter[2]).wait_recv()
-        to_core(section, c, quarter[2]).start()
-
-    each(YL, lambda i: y_copy(1, yl_of(i), yl_of(i)).wait_recv())
-    ds[3] = s2d[1].reshape(ROWS, C)
-    give(ds, dr, d_send, d_recv, 3)
-
-    for section in (left, right, far):
-        for part in range(4):
-            to_core(section, other, part).wait_recv()
+    unless_own(1, relay)
 
     def weight(section, k):
         return w[section, 2 * k : 2 * k + 2].reshape(C, C)
 
     emb_row = emb[pl.ds(p, 1), :]
     for s in range(SECTIONS):
+        unless_own(s, complete)
         x, inv, normed = normalize(hs[s])
         pre = emb_row + dot(before(normed).astype(BF), weight(s, 0))
         pre = pre + dot(normed.astype(BF), weight(s, 1))
@@ -261,6 +263,12 @@
             act = (pre * jax.nn.sigmoid(pre)).astype(BF)
             hs[s + 1] = (x + dot(act, weight(s, 3))).astype(BF)
             give(hs, hr, h_send, h_recv, s + 1)
+        if s + 2 < SECTIONS:
+            unless_own(s + 2, relay)
+        if s == 2:
+            each(YL, lambda i: y_copy(1, yl_of(i), yl_of(i)).wait_recv())
+            ds[3] = s2d[1].reshape(ROWS, C)
+            give(ds, dr, d_send, d_recv, 3)
     for s in (3, 2, 1):
         x, inv, normed = normalize(hs[s])
         grad = ds[s]
@@ -274,16 +282,20 @@
         ds[s - 1] = (grad.astype(F32) + inv * (dnorm - normed * mean)).astype(BF)
         give(ds, dr, d_send, d_recv, s - 1)
 
-    def take(kept, value, send, recv):
-        def one(i):
-            m = x_of(i)
+    def micro(i):
+        return x_of(i + jnp.where(i == 2, 1, 0) - jnp.where(i == 3, 1, 0))
+
+    def taken(kept, value, send, recv, i):
+        m = micro(i)
+
+        @pl.when(i > 0)
+        def _():
             remote(value.at[0], kept.at[m], send.at[0], recv.at[m], at_x(m)).wait_recv()
 
-        each(SECTIONS, one)
-
-    take(hr, hs, h_send, h_recv)
-
-    def redo(m, _):
+        return m
+
+    def redo(i, _):
+        m = taken(hr, hs, h_send, h_recv, i)
         x, inv, normed = normalize(hr[m])
         low = normed.astype(BF)
         pre = emb[pl.ds(m, 1), :] + dot(before(normed).astype(BF), weight(p, 0))
@@ -295,9 +307,9 @@
         return 0
 
     lax.fori_loop(0, SECTIONS, redo, 0)
-    take(dr, ds, d_send, d_recv)
-
-    def redo_back(m, _):
+
+    def redo_back(i, _):
+        m = taken(dr, ds, d_send, d_recv, i)
         pre = pre_s[m]
         sig = jax.nn.sigmoid(pre)
         dpre = dot_t(rhs[3, m], weight(p, 3)) * sig * (1.0 + pre * (1.0 - sig))
@@ -368,7 +380,7 @@
             value = value + ref[i, lo : lo + n].astype(F32)
         return value.astype(BF)
 
-    for q in range(2):
+    for q in range(CHUNKS):
 
         def first(i):
             a1(q, y_of(i), y).start()
@@ -377,7 +389,7 @@
         each(Y, first)
     ra[y] = chip[rows(y * PA, PA), :]
     rbz[z] = chip[rows(HA + z * PB, PB), :]
-    for q in range(2):
+    for q in range(CHUNKS):
         lo, n = CHUNK_A[q]
         each(Y, lambda i: a1(q, y_of(i), y_of(i)).wait_recv())
         ra2[z, lo : lo + n] = total(ra, (lo, n))
@@ -386,7 +398,7 @@
         each(Z, lambda i: b1(q, z_of(i), z_of(i)).wait_recv())
         rb2[y, lo : lo + n] = total(rbz, (lo, n))
         each(Y, lambda i: b2(q, y_of(i), y).start())
-    for q in range(2):
+    for q in range(CHUNKS):
         lo, n = CHUNK_A[q]
         each(Z, lambda i: a2(q, z_of(i), z_of(i)).wait_recv())
         fin[c, rows(y * PA + lo, n), :] = total(ra2, (lo, n))
@@ -400,14 +412,22 @@
         ref = fin.at[core, pl.ds(HA * which, HB if which else HA)]
         return remote(ref, ref, end_sem.at[0, which], end_sem.at[1, which], sibling)
 
-    for q in range(2):
+    def store(core, which):
+        part = pl.ds(HA * which, HB if which else HA)
+        return pltpu.make_async_copy(fin.at[core, part], packed.at[core, part], out_sem.at[core, which])
+
+    for q in range(CHUNKS):
         each(Y, lambda i: a3(q, y_of(i), y_of(i)).wait_recv())
     end(c, 0).start()
-    for q in range(2):
+    store(c, 0).start()
+    for q in range(CHUNKS):
         each(Z, lambda i: b3(q, z_of(i), z_of(i)).wait_recv())
     end(c, 1).start()
+    store(c, 1).start()
     end(other, 0).wait_recv()
+    store(other, 0).start()
     end(other, 1).wait_recv()
+    store(other, 1).start()
 
     for to in (right, left, far):
         over_x(p, to).wait_send()
@@ -427,7 +447,7 @@
 
     each(SECTIONS, left_us)
     swap.wait_send()
-    for q in range(2):
+    for q in range(CHUNKS):
 
         def drained(i):
             a1(q, y_of(i), y).wait_send()
@@ -438,23 +458,34 @@
             b3(q, z_of(i), z).wait_send()
 
         each(Y, drained)
-    end(c, 0).wait_send()
-    end(c, 1).wait_send()
-
-
-def unpack_kernel(scale, fin, conv_out, out_out):
+    for which in range(2):
+        end(c, which).wait_send()
+        store(c, which).wait()
+        store(other, which).wait()
+
+
+def unpack_kernel(scale, packed, conv_out, out_out, fin, full, in_sem, out_sem):
+    loads = [pltpu.make_async_copy(packed.at[core], fin.at[core], in_sem.at[core]) for core in range(2)]
+    for load in loads:
+        load.start()
+    stores = []
     for k in range(4):
-        ref = conv_out.at[0, k] if k < 3 else out_out.at[0]
         core, j = divmod(k, 2)
-        ref[:, 0:128] = fin[core, 2 * j * C : (2 * j + 1) * C, :].astype(F32) * scale
-        ref[:, 128:256] = fin[core, (2 * j + 1) * C : (2 * j + 2) * C, :].astype(F32) * scale
+        if j == 0:
+            loads[core].wait()
+        full[k, :, 0:128] = fin[core, 2 * j * C : (2 * j + 1) * C, :].astype(F32) * scale
+        full[k, :, 128:256] = fin[core, (2 * j + 1) * C : (2 * j + 2) * C, :].astype(F32) * scale
         tail = fin[core, 4 * C : 5 * C, :].astype(F32) * scale
-        ref[:, 256:320] = tail[:, 64 * j : 64 * j + 64]
+        full[k, :, 256:320] = tail[:, 64 * j : 64 * j + 64]
+        to = conv_out.at[0, k] if k < 3 else out_out.at[0]
+        stores.append(pltpu.make_async_copy(full.at[k], to, out_sem.at[k]))
+        stores[k].start()
+    for store in stores:
+        store.wait()
 
 
 def body(video, cotangent, timesteps, conv_weight, out_weight):
     far_memory = pl.BlockSpec(memory_space=pltpu.HBM)
-    vmem = pl.BlockSpec(memory_space=pltpu.VMEM)
     dma = pltpu.SemaphoreType.DMA
     stack = (SECTIONS, ROWS, C)
     rows = video.shape[0] * 4 * 64 * video.shape[3]
@@ -462,7 +493,7 @@
         kernel,
         out_shape=jax.ShapeDtypeStruct((2, HALF, 128), BF),
         in_specs=[far_memory] * 5,
-        out_specs=vmem,
+        out_specs=far_memory,
         scratch_shapes=[
             pltpu.VMEM((2, 64, C), BF),
             pltpu.VMEM((2, 64, C), BF),
@@ -487,6 +518,7 @@
             pltpu.VMEM((8, PB, 128), BF),
             pltpu.VMEM((8, PA, 128), BF),
             pltpu.VMEM((8, PB, 128), BF),
+            pltpu.VMEM((2, HALF, 128), BF),
             dma((5,)),
             dma((Z,)), dma((Z,)), dma((2, YL)), dma((2, YL)),
             dma((SECTIONS,)), dma((SECTIONS,)),
@@ -494,8 +526,8 @@
             dma((SECTIONS,)), dma((SECTIONS,)), dma((SECTIONS,)), dma((SECTIONS,)),
             dma((2,)),
         ]
-        + [dma((2, 8))] * 12
-        + [dma((2, 2))],
+        + [dma((CHUNKS, 8))] * 12
+        + [dma((2, 2))] * 2,
         compiler_params=pltpu.CompilerParams(
             collective_id=1, has_side_effects=True, vmem_limit_bytes=56 << 20
         ),
@@ -513,8 +545,15 @@
             jax.ShapeDtypeStruct((1, 3, C, C), F32),
             jax.ShapeDtypeStruct((1, C, C), F32),
         ),
-        in_specs=[vmem],
-        out_specs=(vmem, vmem),
+        in_specs=[far_memory],
+        out_specs=(far_memory, far_memory),
+        scratch_shapes=[
+            pltpu.VMEM((2, HALF, 128), BF),
+            pltpu.VMEM((4, C, C), F32),
+            dma((2,)),
+            dma((4,)),
+        ],
+        compiler_params=pltpu.CompilerParams(vmem_limit_bytes=56 << 20),
         name="unpack",
     )(packed)
 

time: 77.1 us -> 73.7 us (0.956)
  Pallas kernels: 76.2 us -> 72.9 us
    pallas_call x1, Pallas kernels: 73.6 us -> 70.5 us  [body(): pl.pallas_call(kernel, out_shape=jax.ShapeDtypeStruct((2, HALF, 128), BF)...]
where the time goes in v3:
time: 73.7 us; the launch traced here: 73.5 us
  Pallas kernels  72.9 us (99%)
    pallas_call x1, Pallas kernels, body(): pl.pallas_call(kernel, out_shape=jax.ShapeDtypeStruct((2, HALF, 128), BF)...  70.5 us
    pallas_call x1, Pallas kernels, body(): pl.pallas_call(functools.partial(unpack_kernel, 1.0 / math.sqrt(rows)), o...  2.37 us

profile of v3, /device:TPU:1, one launch (start us, length us, event | category | flops | bytes accessed | tf_op | source)
XLA Modules:
  0.0 73.5 jit_solution(15207326084899252220)
XLA Ops:
  0.6 70.5 %main.1.packed = bf16[2,1664,128]{2,1,0:T(8,128)(2,1)} custom-call(bf16[4,1,2,64,320]{4,3,2,1,0:T(8,128)(2,1)} %video.1, bf16[4,1,2,64,320]{4,3,2,1,0:T(8,128)(2,1)} %cotangent.1, s32[1,4]{1,0:T(1,128)} %bitcast.5, bf16[1,6,160,320]{3,2,1,0:T(8,128)(2,1)} %bitcast.3, bf16[1,2,160,320]{3,2,1,0:T(8,128)(2,1)} %bitcast.4), custom_call_target="tpu_custom_call" | custom-call | tf_op jit(solution)/shard_map/main/pallas_call | solution.py:492
  71.1 2.4 %unpack.1 = (f32[1,3,320,320]{3,2,1,0:T(8,128)}, f32[1,320,320]{2,1,0:T(8,128)}) custom-call(bf16[2,1664,128]{2,1,0:T(8,128)(2,1)} %main.1.packed), custom_call_target="tpu_custom_call" | custom-call | tf_op jit(solution)/shard_map/unpack/pallas_call | solution.py:542

commit v4 on v3

--- a/solution.py
+++ b/solution.py
@@ -19,6 +19,7 @@
 HALF = HA + HB
 CHUNK_A, CHUNK_B = ((0, 48), (48, 32), (80, 32)), ((0, 32), (32, 32), (64, 32))
 CHUNKS = 3
+WIDE = 2 * ROWS + ROWS // 2
 QUARTER = C // 2
 BF = jnp.bfloat16
 F32 = jnp.float32
@@ -92,7 +93,7 @@
 
 def kernel(
     video, cotangent, times, convw, outw, packed,
-    vin, cin, tin, emb, w, s1s, s1d, s2s, s2d, hs, ds, pre_s, hr, lhs, rhs,
+    vin, cin, tin, emb, w, s1s, s1d, s2s, s2d, hs, ds, slope, dense, hr, dr, lhs, rhs,
     gown, sb, rb, chip, ra, rbz, ra2, rb2, fin,
     in_sem, z_send, z_recv, y_send, y_recv,
     x_send, x_recv, n_send, n_recv, c_send, c_recv,
@@ -103,6 +104,36 @@
     yl = lax.rem(y, YL)
     ybase = y - yl
     other = 1 - c
+    barrier = pltpu.get_barrier_semaphore()
+
+    def greet(to):
+        pl.semaphore_signal(barrier, inc=1, device_id=to, device_id_type=MESH)
+
+    def at_x(to):
+        return device(to, y, z, c)
+
+    def at_y(to):
+        return device(p, to, z, c)
+
+    def at_z(to):
+        return device(p, y, to, c)
+
+    def x_of(i):
+        return lax.rem(p + i, SECTIONS)
+
+    def y_of(i):
+        return lax.rem(y + i, Y)
+
+    def z_of(i):
+        return lax.rem(z + i, Z)
+
+    sibling = device(p, y, z, other)
+    for i in (4, 3, 5, 2, 6, 1, 7):
+        greet(at_y(y_of(i)))
+        greet(at_z(z_of(i)))
+    for i in (2, 1, 3):
+        greet(at_x(x_of(i)))
+    greet(sibling)
     loads = [
         pltpu.make_async_copy(convw.at[0], w.at[p, pl.ds(0, 6)], in_sem.at[2]),
         pltpu.make_async_copy(outw.at[0], w.at[p, pl.ds(6, 2)], in_sem.at[3]),
@@ -113,36 +144,13 @@
     for load in loads:
         load.start()
 
-    barrier = pltpu.get_barrier_semaphore()
-
-    def greet(to):
-        pl.semaphore_signal(barrier, inc=1, device_id=to, device_id_type=MESH)
-
-    def at_x(to):
-        return device(to, y, z, c)
-
-    def at_y(to):
-        return device(p, to, z, c)
-
-    def at_z(to):
-        return device(p, y, to, c)
-
-    def x_of(i):
-        return lax.rem(p + i, SECTIONS)
-
-    def y_of(i):
-        return lax.rem(y + i, Y)
-
-    def z_of(i):
-        return lax.rem(z + i, Z)
-
-    sibling = device(p, y, z, other)
-    each(SECTIONS, lambda i: greet(at_x(x_of(i))))
-    each(Y, lambda i: greet(at_y(y_of(i))))
-    each(Z, lambda i: greet(at_z(z_of(i))))
-    greet(sibling)
     for load in loads:
         load.wait()
+
+    def by_z(kind, ref):
+        s1s[kind] = reorder(to_z, ref[...].reshape(ROWS, C)).reshape(Z, 16, C)
+
+    by_z(0, vin)
     pl.semaphore_wait(barrier, SECTIONS + Y + Z - 3 + 1)
 
     color = lax.rem((y + 2 * z) * other + (2 * y + z) * c, 4)
@@ -173,14 +181,17 @@
     for to in (jnp.where(first, far, right), jnp.where(first, right, left), jnp.where(first, left, far)):
         over_x(p, to).start()
 
-    s1s[:, 0:16, :] = reorder(to_z, vin[...].reshape(ROWS, C)).reshape(Z, 16, C)
-    s1s[:, 16:32, :] = reorder(to_z, cin[...].reshape(ROWS, C)).reshape(Z, 16, C)
-
-    def z_copy(at, slot):
-        return remote(s1s.at[at], s1d.at[slot], z_send.at[at], z_recv.at[slot], at_z(at))
-
-    each(Z, lambda i: z_copy(z_of(i), z).start())
-    s1d[z] = s1s[z]
+    def z_copy(kind, at, slot):
+        return remote(
+            s1s.at[kind, at], s1d.at[kind, slot], z_send.at[kind, at], z_recv.at[kind, slot], at_z(at)
+        )
+
+    for kind in range(2):
+        if kind:
+            by_z(1, cin)
+        for i in (4, 3, 5, 2, 6, 1, 7):
+            z_copy(kind, z_of(i), z).start()
+        s1d[kind, z] = s1s[kind, z]
 
     lane = lax.broadcasted_iota(jnp.int32, (1, C), 1)
     index = jnp.where(lane < C // 2, lane, lane - C // 2).astype(F32)
@@ -214,8 +225,6 @@
     unless_own(0, spread)
     unless_own(1, spread)
 
-    each(Z, lambda i: z_copy(z_of(i), z_of(i)).wait_recv())
-
     def yl_of(i):
         return lax.rem(yl + i, YL)
 
@@ -225,9 +234,13 @@
         )
 
     for kind in range(2):
-        s2s[kind] = reorder(to_y, s1d[:, 16 * kind : 16 * kind + 16, :].reshape(ROWS, C)).reshape(YL, 32, C)
+        each(Z, lambda i: z_copy(kind, z_of(i), z_of(i)).wait_recv())
+        s2s[kind] = reorder(to_y, s1d[kind].reshape(ROWS, C)).reshape(YL, 32, C)
+        if kind:
+            unless_own(3, spread)
         each(YL, lambda i: y_copy(kind, yl_of(i), yl).start())
-        unless_own(2 + kind, spread)
+        if not kind:
+            unless_own(2, spread)
         s2d[kind, yl] = s2s[kind, yl]
 
     def give(value, kept, send, recv, section):
@@ -241,7 +254,15 @@
         def _():
             kept[p] = value[section]
 
-    dr = rhs.at[3]
+    def give_dense(section, value):
+        low = value[:, 256:320]
+        dense[section, 0:ROWS] = value[:, 0:128].astype(BF)
+        dense[section, ROWS : 2 * ROWS] = value[:, 128:256].astype(BF)
+        dense[section, 2 * ROWS : WIDE] = jnp.concatenate(
+            [low[0 : ROWS // 2], low[ROWS // 2 : ROWS]], 1
+        ).astype(BF)
+        give(dense, dr, d_send, d_recv, section)
+
     unless_own(0, relay)
     each(YL, lambda i: y_copy(0, yl_of(i), yl_of(i)).wait_recv())
     hs[0] = s2d[0].reshape(ROWS, C)
@@ -258,9 +279,10 @@
         pre = emb_row + dot(before(normed).astype(BF), weight(s, 0))
         pre = pre + dot(normed.astype(BF), weight(s, 1))
         pre = pre + dot(after(normed).astype(BF), weight(s, 2))
-        pre_s[s] = pre
+        sig = jax.nn.sigmoid(pre)
+        slope[s] = sig * (1.0 + pre * (1.0 - sig))
         if s + 1 < SECTIONS:
-            act = (pre * jax.nn.sigmoid(pre)).astype(BF)
+            act = (pre * sig).astype(BF)
             hs[s + 1] = (x + dot(act, weight(s, 3))).astype(BF)
             give(hs, hr, h_send, h_recv, s + 1)
         if s + 2 < SECTIONS:
@@ -268,19 +290,19 @@
         if s == 2:
             each(YL, lambda i: y_copy(1, yl_of(i), yl_of(i)).wait_recv())
             ds[3] = s2d[1].reshape(ROWS, C)
-            give(ds, dr, d_send, d_recv, 3)
+            give_dense(3, ds[3].astype(F32))
     for s in (3, 2, 1):
         x, inv, normed = normalize(hs[s])
         grad = ds[s]
-        pre = pre_s[s]
-        sig = jax.nn.sigmoid(pre)
-        dpre = dot_t(grad, weight(s, 3)) * sig * (1.0 + pre * (1.0 - sig))
+        dpre = dot_t(grad, weight(s, 3)) * slope[s]
         dnorm = dot_t(after(dpre).astype(BF), weight(s, 0))
         dnorm = dnorm + dot_t(dpre.astype(BF), weight(s, 1))
         dnorm = dnorm + dot_t(before(dpre).astype(BF), weight(s, 2))
         mean = jnp.mean(dnorm * normed, -1, keepdims=True)
-        ds[s - 1] = (grad.astype(F32) + inv * (dnorm - normed * mean)).astype(BF)
-        give(ds, dr, d_send, d_recv, s - 1)
+        result = grad.astype(F32) + inv * (dnorm - normed * mean)
+        give_dense(s - 1, result)
+        if s > 1:
+            ds[s - 1] = result.astype(BF)
 
     def micro(i):
         return x_of(i + jnp.where(i == 2, 1, 0) - jnp.where(i == 3, 1, 0))
@@ -301,18 +323,22 @@
         pre = emb[pl.ds(m, 1), :] + dot(before(normed).astype(BF), weight(p, 0))
         pre = pre + dot(low, weight(p, 1))
         pre = pre + dot(after(normed).astype(BF), weight(p, 2))
-        pre_s[m] = pre
+        sig = jax.nn.sigmoid(pre)
+        slope[m] = sig * (1.0 + pre * (1.0 - sig))
         lhs[0, m] = low
-        lhs[1, m] = (pre * jax.nn.sigmoid(pre)).astype(BF)
+        lhs[1, m] = (pre * sig).astype(BF)
         return 0
 
     lax.fori_loop(0, SECTIONS, redo, 0)
 
     def redo_back(i, _):
-        m = taken(dr, ds, d_send, d_recv, i)
-        pre = pre_s[m]
-        sig = jax.nn.sigmoid(pre)
-        dpre = dot_t(rhs[3, m], weight(p, 3)) * sig * (1.0 + pre * (1.0 - sig))
+        m = taken(dr, dense, d_send, d_recv, i)
+        low = dr[m, 2 * ROWS : WIDE].astype(F32)
+        low = jnp.concatenate([low[:, 0:64], low[:, 64:128]], 0).astype(BF)
+        rhs[3, m, :, 0:128] = dr[m, 0:ROWS]
+        rhs[3, m, :, 128:256] = dr[m, ROWS : 2 * ROWS]
+        rhs[3, m, :, 256:320] = low
+        dpre = dot_t(rhs[3, m], weight(p, 3)) * slope[m]
         rhs[0, m] = after(dpre).astype(BF)
         rhs[1, m] = dpre.astype(BF)
         rhs[2, m] = before(dpre).astype(BF)
@@ -320,7 +346,7 @@
 
     lax.fori_loop(0, SECTIONS, redo_back, 0)
 
-    def gradients(core, ref):
+    def gradients(core, ref, then):
         tails = []
         for j in range(2):
             k = 2 * core + j
@@ -330,15 +356,20 @@
             ref[2 * j * C : (2 * j + 1) * C, :] = term[:, 0:128].astype(ref.dtype)
             ref[(2 * j + 1) * C : (2 * j + 2) * C, :] = term[:, 128:256].astype(ref.dtype)
             tails.append(term[:, 256:320])
-        ref[4 * C : 5 * C, :] = jnp.concatenate(tails, 1).astype(ref.dtype)
-        ref[5 * C : HALF, :] = jnp.zeros((HALF - 5 * C, 128), ref.dtype)
-
-    gradients(other, sb)
-    swap = remote(sb, rb, core_sem.at[0], core_sem.at[1], sibling)
-    swap.start()
-    gradients(c, gown)
-    swap.wait_recv()
-    chip[...] = (gown[...] + rb[...].astype(F32)).astype(BF)
+            if j:
+                ref[4 * C : 5 * C, :] = jnp.concatenate(tails, 1).astype(ref.dtype)
+                ref[5 * C : HALF, :] = jnp.zeros((HALF - 5 * C, 128), ref.dtype)
+            then(j)
+
+    def swap(j):
+        part = pl.ds(2 * C * j, HALF - 2 * C if j else 2 * C)
+        return remote(sb.at[part], rb.at[part], core_sem.at[0, j], core_sem.at[1, j], sibling)
+
+    gradients(other, sb, lambda j: swap(j).start())
+    gradients(c, gown, lambda j: None)
+    for j, (lo, hi) in enumerate(((0, 2 * C), (2 * C, HALF))):
+        swap(j).wait_recv()
+        chip[lo:hi] = (gown[lo:hi] + rb[lo:hi].astype(F32)).astype(BF)
 
     def rows(start, size):
         return pl.ds(pl.multiple_of(start, 16), size)
@@ -436,17 +467,18 @@
             to_next(section, way, color).wait_send()
         for part in range(4):
             to_core(section, c, part).wait_send()
-    each(Z, lambda i: z_copy(z_of(i), z).wait_send())
     for kind in range(2):
+        each(Z, lambda i: z_copy(kind, z_of(i), z).wait_send())
         each(YL, lambda i: y_copy(kind, yl_of(i), yl).wait_send())
 
     def left_us(i):
         s = x_of(i)
         remote(hs.at[s], hr.at[p], h_send.at[s], h_recv.at[p], at_x(s)).wait_send()
-        remote(ds.at[s], dr.at[p], d_send.at[s], d_recv.at[p], at_x(s)).wait_send()
+        remote(dense.at[s], dr.at[p], d_send.at[s], d_recv.at[p], at_x(s)).wait_send()
 
     each(SECTIONS, left_us)
-    swap.wait_send()
+    swap(0).wait_send()
+    swap(1).wait_send()
     for q in range(CHUNKS):
 
         def drained(i):
@@ -500,14 +532,16 @@
             pltpu.VMEM((1, SECTIONS), jnp.int32),
             pltpu.VMEM((SECTIONS, C), F32),
             pltpu.VMEM((SECTIONS, 8, QUARTER, C), BF),
-            pltpu.VMEM((Z, 32, C), BF),
-            pltpu.VMEM((Z, 32, C), BF),
+            pltpu.VMEM((2, Z, 16, C), BF),
+            pltpu.VMEM((2, Z, 16, C), BF),
             pltpu.VMEM((2, YL, 32, C), BF),
             pltpu.VMEM((2, YL, 32, C), BF),
             pltpu.VMEM(stack, BF),
             pltpu.VMEM(stack, BF),
             pltpu.VMEM(stack, F32),
+            pltpu.VMEM((SECTIONS, WIDE, 128), BF),
             pltpu.VMEM(stack, BF),
+            pltpu.VMEM((SECTIONS, WIDE, 128), BF),
             pltpu.VMEM((2, *stack), BF),
             pltpu.VMEM((4, *stack), BF),
             pltpu.VMEM((HALF, 128), F32),
@@ -520,11 +554,11 @@
             pltpu.VMEM((8, PB, 128), BF),
             pltpu.VMEM((2, HALF, 128), BF),
             dma((5,)),
-            dma((Z,)), dma((Z,)), dma((2, YL)), dma((2, YL)),
+            dma((2, Z)), dma((2, Z)), dma((2, YL)), dma((2, YL)),
             dma((SECTIONS,)), dma((SECTIONS,)),
             dma((SECTIONS, 4)), dma((SECTIONS, 4)), dma((SECTIONS, 4)), dma((SECTIONS, 4)),
             dma((SECTIONS,)), dma((SECTIONS,)), dma((SECTIONS,)), dma((SECTIONS,)),
-            dma((2,)),
+            dma((2, 2)),
         ]
         + [dma((CHUNKS, 8))] * 12
         + [dma((2, 2))] * 2,

time: 73.7 us -> 73 us (level)
  no operation moved by 1% of the time
where the time goes in v4:
time: 73 us; the launch traced here: 72.8 us
  Pallas kernels  72.2 us (99%)
    pallas_call x1, Pallas kernels, body(): pl.pallas_call(kernel, out_shape=jax.ShapeDtypeStruct((2, HALF, 128), BF)...  69.8 us
    pallas_call x1, Pallas kernels, body(): pl.pallas_call(functools.partial(unpack_kernel, 1.0 / math.sqrt(rows)), o...  2.37 us

profile of v4, /device:TPU:1, one launch (start us, length us, event | category | flops | bytes accessed | tf_op | source)
XLA Modules:
  0.0 72.8 jit_solution(16281189580966641115)
XLA Ops:
  0.6 69.8 %main.1.packed = bf16[2,1664,128]{2,1,0:T(8,128)(2,1)} custom-call(bf16[4,1,2,64,320]{4,3,2,1,0:T(8,128)(2,1)} %video.1, bf16[4,1,2,64,320]{4,3,2,1,0:T(8,128)(2,1)} %cotangent.1, s32[1,4]{1,0:T(1,128)} %bitcast.5, bf16[1,6,160,320]{3,2,1,0:T(8,128)(2,1)} %bitcast.3, bf16[1,2,160,320]{3,2,1,0:T(8,128)(2,1)} %bitcast.4), custom_call_target="tpu_custom_call" | custom-call | tf_op jit(solution)/shard_map/main/pallas_call | solution.py:524
  70.4 2.4 %unpack.1 = (f32[1,3,320,320]{3,2,1,0:T(8,128)}, f32[1,320,320]{2,1,0:T(8,128)}) custom-call(bf16[2,1664,128]{2,1,0:T(8,128)(2,1)} %main.1.packed), custom_call_target="tpu_custom_call" | custom-call | tf_op jit(solution)/shard_map/unpack/pallas_call | solution.py:576

commit v5 on v4

--- a/solution.py
+++ b/solution.py
@@ -46,6 +46,10 @@
         return 0
 
     lax.fori_loop(1, count, step, 0)
+
+
+def far_first(fn):
+    each(8, lambda i: fn(4 + lax.div(i, 2) * (2 * lax.rem(i, 2) - 1)))
 
 
 def dot(a, b):
@@ -153,8 +157,8 @@
     by_z(0, vin)
     pl.semaphore_wait(barrier, SECTIONS + Y + Z - 3 + 1)
 
-    color = lax.rem((y + 2 * z) * other + (2 * y + z) * c, 4)
-    step_y, step_z = other, c
+    color = lax.rem(2 * y + z, 4)
+    step_y, step_z = 0, 1
     nexts = [
         device(p, lax.rem(y + step_y, Y), lax.rem(z + step_z, Z), c),
         device(p, lax.rem(y + Y - step_y, Y), lax.rem(z + Z - step_z, Z), c),
@@ -234,10 +238,10 @@
         )
 
     for kind in range(2):
+        if kind:
+            unless_own(3, spread)
         each(Z, lambda i: z_copy(kind, z_of(i), z_of(i)).wait_recv())
         s2s[kind] = reorder(to_y, s1d[kind].reshape(ROWS, C)).reshape(YL, 32, C)
-        if kind:
-            unless_own(3, spread)
         each(YL, lambda i: y_copy(kind, yl_of(i), yl).start())
         if not kind:
             unless_own(2, spread)
@@ -417,27 +421,27 @@
             a1(q, y_of(i), y).start()
             b1(q, z_of(i), z).start()
 
-        each(Y, first)
+        far_first(first)
     ra[y] = chip[rows(y * PA, PA), :]
     rbz[z] = chip[rows(HA + z * PB, PB), :]
     for q in range(CHUNKS):
         lo, n = CHUNK_A[q]
         each(Y, lambda i: a1(q, y_of(i), y_of(i)).wait_recv())
         ra2[z, lo : lo + n] = total(ra, (lo, n))
-        each(Z, lambda i: a2(q, z_of(i), z).start())
+        far_first(lambda i: a2(q, z_of(i), z).start())
         lo, n = CHUNK_B[q]
         each(Z, lambda i: b1(q, z_of(i), z_of(i)).wait_recv())
         rb2[y, lo : lo + n] = total(rbz, (lo, n))
-        each(Y, lambda i: b2(q, y_of(i), y).start())
+        far_first(lambda i: b2(q, y_of(i), y).start())
     for q in range(CHUNKS):
         lo, n = CHUNK_A[q]
         each(Z, lambda i: a2(q, z_of(i), z_of(i)).wait_recv())
         fin[c, rows(y * PA + lo, n), :] = total(ra2, (lo, n))
-        each(Y, lambda i: a3(q, y_of(i), y).start())
+        far_first(lambda i: a3(q, y_of(i), y).start())
         lo, n = CHUNK_B[q]
         each(Y, lambda i: b2(q, y_of(i), y_of(i)).wait_recv())
         fin[c, rows(HA + z * PB + lo, n), :] = total(rb2, (lo, n))
-        each(Z, lambda i: b3(q, z_of(i), z).start())
+        far_first(lambda i: b3(q, z_of(i), z).start())
 
     def end(core, which):
         ref = fin.at[core, pl.ds(HA * which, HB if which else HA)]

time: 73 us -> 71.4 us (0.978)
  Pallas kernels: 72.2 us -> 70.6 us
    pallas_call x1, Pallas kernels: 69.8 us -> 68.2 us  [body(): pl.pallas_call(kernel, out_shape=jax.ShapeDtypeStruct((2, HALF, 128), BF)...]
where the time goes in v5:
time: 71.4 us; the launch traced here: 71.2 us
  Pallas kernels  70.6 us (99%)
    pallas_call x1, Pallas kernels, body(): pl.pallas_call(kernel, out_shape=jax.ShapeDtypeStruct((2, HALF, 128), BF)...  68.2 us
    pallas_call x1, Pallas kernels, body(): pl.pallas_call(functools.partial(unpack_kernel, 1.0 / math.sqrt(rows)), o...  2.37 us

profile of v5, /device:TPU:1, one launch (start us, length us, event | category | flops | bytes accessed | tf_op | source)
XLA Modules:
  0.0 71.2 jit_solution(14339676557369405426)
XLA Ops:
  0.6 68.2 %main.1.packed = bf16[2,1664,128]{2,1,0:T(8,128)(2,1)} custom-call(bf16[4,1,2,64,320]{4,3,2,1,0:T(8,128)(2,1)} %video.1, bf16[4,1,2,64,320]{4,3,2,1,0:T(8,128)(2,1)} %cotangent.1, s32[1,4]{1,0:T(1,128)} %bitcast.5, bf16[1,6,160,320]{3,2,1,0:T(8,128)(2,1)} %bitcast.3, bf16[1,2,160,320]{3,2,1,0:T(8,128)(2,1)} %bitcast.4), custom_call_target="tpu_custom_call" | custom-call | tf_op jit(solution)/shard_map/main/pallas_call | solution.py:528
  68.9 2.4 %unpack.1 = (f32[1,3,320,320]{3,2,1,0:T(8,128)}, f32[1,320,320]{2,1,0:T(8,128)}) custom-call(bf16[2,1664,128]{2,1,0:T(8,128)(2,1)} %main.1.packed), custom_call_target="tpu_custom_call" | custom-call | tf_op jit(solution)/shard_map/unpack/pallas_call | solution.py:580

commit v6 on v5

--- a/solution.py
+++ b/solution.py
@@ -97,7 +97,7 @@
 
 def kernel(
     video, cotangent, times, convw, outw, packed,
-    vin, cin, tin, emb, w, s1s, s1d, s2s, s2d, hs, ds, slope, dense, hr, dr, lhs, rhs,
+    vin, cin, tin, emb, w, s1s, s1d, s2s, s2d, hs, ds, slope, dense, packed_h, hr, dr, lhs, rhs,
     gown, sb, rb, chip, ra, rbz, ra2, rb2, fin,
     in_sem, z_send, z_recv, y_send, y_recv,
     x_send, x_recv, n_send, n_recv, c_send, c_recv,
@@ -258,19 +258,26 @@
         def _():
             kept[p] = value[section]
 
-    def give_dense(section, value):
+    def pack(ref, section, value):
         low = value[:, 256:320]
-        dense[section, 0:ROWS] = value[:, 0:128].astype(BF)
-        dense[section, ROWS : 2 * ROWS] = value[:, 128:256].astype(BF)
-        dense[section, 2 * ROWS : WIDE] = jnp.concatenate(
+        ref[section, 0:ROWS] = value[:, 0:128].astype(BF)
+        ref[section, ROWS : 2 * ROWS] = value[:, 128:256].astype(BF)
+        ref[section, 2 * ROWS : WIDE] = jnp.concatenate(
             [low[0 : ROWS // 2], low[ROWS // 2 : ROWS]], 1
         ).astype(BF)
+
+    def give_dense(section, value):
+        pack(dense, section, value)
         give(dense, dr, d_send, d_recv, section)
+
+    def give_hidden(section, value):
+        pack(packed_h, section, value)
+        give(packed_h, hr, h_send, h_recv, section)
 
     unless_own(0, relay)
     each(YL, lambda i: y_copy(0, yl_of(i), yl_of(i)).wait_recv())
     hs[0] = s2d[0].reshape(ROWS, C)
-    give(hs, hr, h_send, h_recv, 0)
+    give_hidden(0, hs[0].astype(F32))
     unless_own(1, relay)
 
     def weight(section, k):
@@ -287,8 +294,9 @@
         slope[s] = sig * (1.0 + pre * (1.0 - sig))
         if s + 1 < SECTIONS:
             act = (pre * sig).astype(BF)
-            hs[s + 1] = (x + dot(act, weight(s, 3))).astype(BF)
-            give(hs, hr, h_send, h_recv, s + 1)
+            result = x + dot(act, weight(s, 3))
+            give_hidden(s + 1, result)
+            hs[s + 1] = result.astype(BF)
         if s + 2 < SECTIONS:
             unless_own(s + 2, relay)
         if s == 2:
@@ -321,8 +329,11 @@
         return m
 
     def redo(i, _):
-        m = taken(hr, hs, h_send, h_recv, i)
-        x, inv, normed = normalize(hr[m])
+        m = taken(hr, packed_h, h_send, h_recv, i)
+        low = hr[m, 2 * ROWS : WIDE].astype(F32)
+        low = jnp.concatenate([low[:, 0:64], low[:, 64:128]], 0)
+        wide = [hr[m, 0:ROWS].astype(F32), hr[m, ROWS : 2 * ROWS].astype(F32), low]
+        x, inv, normed = normalize(jnp.concatenate(wide, 1))
         low = normed.astype(BF)
         pre = emb[pl.ds(m, 1), :] + dot(before(normed).astype(BF), weight(p, 0))
         pre = pre + dot(low, weight(p, 1))
@@ -477,7 +488,7 @@
 
     def left_us(i):
         s = x_of(i)
-        remote(hs.at[s], hr.at[p], h_send.at[s], h_recv.at[p], at_x(s)).wait_send()
+        remote(packed_h.at[s], hr.at[p], h_send.at[s], h_recv.at[p], at_x(s)).wait_send()
         remote(dense.at[s], dr.at[p], d_send.at[s], d_recv.at[p], at_x(s)).wait_send()
 
     each(SECTIONS, left_us)
@@ -544,7 +555,8 @@
             pltpu.VMEM(stack, BF),
             pltpu.VMEM(stack, F32),
             pltpu.VMEM((SECTIONS, WIDE, 128), BF),
-            pltpu.VMEM(stack, BF),
+            pltpu.VMEM((SECTIONS, WIDE, 128), BF),
+            pltpu.VMEM((SECTIONS, WIDE, 128), BF),
             pltpu.VMEM((SECTIONS, WIDE, 128), BF),
             pltpu.VMEM((2, *stack), BF),
             pltpu.VMEM((4, *stack), BF),

time: 71.4 us -> 71.8 us (level)
  no operation moved by 1% of the time
where the time goes in v6:
time: 71.8 us; the launch traced here: 71.6 us
  Pallas kernels  71 us (99%)
    pallas_call x1, Pallas kernels, body(): pl.pallas_call(kernel, out_shape=jax.ShapeDtypeStruct((2, HALF, 128), BF)...  68.6 us
    pallas_call x1, Pallas kernels, body(): pl.pallas_call(functools.partial(unpack_kernel, 1.0 / math.sqrt(rows)), o...  2.37 us

profile of v6, /device:TPU:1, one launch (start us, length us, event | category | flops | bytes accessed | tf_op | source)
XLA Modules:
  0.0 71.6 jit_solution(3804975209125392141)
XLA Ops:
  0.6 68.6 %main.1.packed = bf16[2,1664,128]{2,1,0:T(8,128)(2,1)} custom-call(bf16[4,1,2,64,320]{4,3,2,1,0:T(8,128)(2,1)} %video.1, bf16[4,1,2,64,320]{4,3,2,1,0:T(8,128)(2,1)} %cotangent.1, s32[1,4]{1,0:T(1,128)} %bitcast.5, bf16[1,6,160,320]{3,2,1,0:T(8,128)(2,1)} %bitcast.3, bf16[1,2,160,320]{3,2,1,0:T(8,128)(2,1)} %bitcast.4), custom_call_target="tpu_custom_call" | custom-call | tf_op jit(solution)/shard_map/main/pallas_call | solution.py:539
  69.3 2.4 %unpack.1 = (f32[1,3,320,320]{3,2,1,0:T(8,128)}, f32[1,320,320]{2,1,0:T(8,128)}) custom-call(bf16[2,1664,128]{2,1,0:T(8,128)(2,1)} %main.1.packed), custom_call_target="tpu_custom_call" | custom-call | tf_op jit(solution)/shard_map/unpack/pallas_call | solution.py:592
